TPU v7x, 256 devices: a whole 4x4x8 slice. The times are simulated.
256 devices in a mesh: seq: 64 (over z, x, core), head: 4 (over y).
Axes of the slice: x: 4, y: 4, z: 8, core: 2. Of those that a mesh axis runs over, the one named last changes fastest.
Arguments:
- queries: bfloat16 [8192, 4096], P(('seq', 'head')), may hold values from -6 to 6
- keys: bfloat16 [8192, 4096], P(('seq', 'head')), may hold values from -6 to 6
- values: bfloat16 [8192, 4096], P(('seq', 'head')), may hold values from -6 to 6
- grad_out: bfloat16 [8192, 4096], P(('seq', 'head')), may hold values from -6 to 6
- random_blocks: int32 [32, 128, 3], replicated, may hold values from 0 to 127, as said below
- global_blocks: int32 [2], replicated, may hold values from 0 to 127
Outputs:
- attended: bfloat16 [8192, 4096], P(('seq', 'head'))
- grad_queries: bfloat16 [8192, 4096], P(('seq', 'head'))
- grad_keys: bfloat16 [8192, 4096], P(('seq', 'head'))
- grad_values: bfloat16 [8192, 4096], P(('seq', 'head'))
Inputs may be any that keep to these rules, and one draw needn't show every extreme that they name: `random_blocks`: for the heads of one index of head and the query blocks of one index of seq, at most 2 random entries lie in the blocks of any one index of seq, and in every such group some index of seq holds exactly 2.
All inputs are finite; a program needn't handle non-finite values.
Results may differ from a plain program's by a relative error of at most 0.034.
Values may be sent and summed in bfloat16 or wider, within the bound.
A program may use at most 128 MiB of HBM per device.

v0:
```python
import jax
import jax.numpy as jnp
from jax import lax
from jax.sharding import PartitionSpec as P

HEAD_DIM = 128
BLOCK = 64
RAND_BLOCKS = 3
GLOB_BLOCKS = 2


def extended(shard, sides, width):
    for axis, dim in sides:
        devices, length = (lax.axis_size(axis), shard.shape[dim])
        up = [(i, (i + 1) % devices) for i in range(devices - 1)]
        down = [(j, i) for i, j in up]
        last = lax.slice_in_dim(shard, length - width, length, axis=dim)
        first = lax.slice_in_dim(shard, 0, width, axis=dim)
        before = lax.ppermute(last, axis, up)
        after = lax.ppermute(first, axis, down)
        shard = jnp.concatenate([before, shard, after], axis=dim)
    return shard


def spread_2(shard, axis, root):
    mine = lax.axis_index(axis) == root
    return lax.psum(jnp.where(mine, shard, jnp.zeros_like(shard)), axis)


def product(formula, former, latter):
    return jnp.einsum(formula, former, latter, preferred_element_type=jnp.float32)


def spread(near_part, offset):
    widths = [(0, 0), (offset, 2 - offset), (0, 0), (0, 0), (0, 0)]
    return jnp.pad(near_part, widths)


def body(queries, keys, values, grad_out, random_blocks, global_blocks):
    score_scale = HEAD_DIM ** (-0.5)
    query_rows, key_rows, value_rows, upstream_rows = (
        lax.all_to_all(queries, "head", split_axis=1, concat_axis=0, tiled=True),
        lax.all_to_all(keys, "head", split_axis=1, concat_axis=0, tiled=True),
        lax.all_to_all(values, "head", split_axis=1, concat_axis=0, tiled=True),
        lax.all_to_all(grad_out, "head", split_axis=1, concat_axis=0, tiled=True),
    )
    tokens_here, width_here = query_rows.shape
    heads_here = width_here // HEAD_DIM
    blocks_here = tokens_here // BLOCK
    shards = lax.axis_size("seq")
    my_shard = lax.axis_index("seq")
    my_group = lax.axis_index("head")
    tile_shape = (blocks_here, BLOCK, heads_here, HEAD_DIM)
    query_tiles = query_rows.reshape(tile_shape)
    incoming_gradient = upstream_rows.reshape(tile_shape)
    pair_rows = jnp.stack([key_rows, value_rows])
    widened = extended(pair_rows, (("seq", 1),), BLOCK)
    widened = widened.reshape((2, blocks_here + 2) + tile_shape[1:])
    window = jnp.stack([widened[:, :-2], widened[:, 1:-1], widened[:, 2:]], axis=2)
    total_blocks = shards * blocks_here
    block_ids = my_shard * blocks_here + jnp.arange(blocks_here, dtype=jnp.int32)
    window_ok = jnp.stack([block_ids >= 1, block_ids >= 0, block_ids + 1 < total_blocks], axis=1)
    pair_tiles = pair_rows.reshape((2,) + tile_shape)
    fetched = []
    for glob_index in range(GLOB_BLOCKS):
        target = global_blocks[glob_index]
        global_tile = lax.dynamic_index_in_dim(pair_tiles, target % blocks_here, 1, keepdims=False)
        fetched.append(spread_2(global_tile, "seq", target // blocks_here))
    global_pair = jnp.stack(fetched, axis=1)
    requests = heads_here * blocks_here * RAND_BLOCKS
    slot_count = max(2, requests // shards + 1)
    request_table = lax.dynamic_slice_in_dim(random_blocks, my_group * heads_here, heads_here, 0)
    request_table = (
        request_table.reshape(heads_here, shards, blocks_here, RAND_BLOCKS)
        .transpose(1, 0, 2, 3)
        .reshape(shards, requests)
    )
    owners = request_table // blocks_here
    positions = jnp.arange(requests, dtype=jnp.int32)
    tile_ids = positions // (blocks_here * RAND_BLOCKS) * blocks_here + request_table % blocks_here
    to_me = (owners == my_shard).astype(jnp.int32)
    order_out = jnp.cumsum(to_me, axis=1) - to_me
    slot_ids = jnp.arange(slot_count, dtype=jnp.int32)
    chosen = (to_me[:, None, :] == 1) & (order_out[:, None, :] == slot_ids[None, :, None])
    slot_used = jnp.any(chosen, axis=2)
    send_ids = jnp.sum(jnp.where(chosen, tile_ids[:, None, :], 0), axis=2)
    send_block = send_ids % blocks_here
    send_head = send_ids // blocks_here
    slot_mask = slot_used[:, :, None, None]
    key_send = jnp.where(
        slot_mask, pair_tiles[0][send_block, :, send_head, :], jnp.zeros((), jnp.bfloat16)
    )
    value_send = jnp.where(
        slot_mask, pair_tiles[1][send_block, :, send_head, :], jnp.zeros((), jnp.bfloat16)
    )
    key_recv, value_recv = (
        lax.all_to_all(key_send, "seq", split_axis=0, concat_axis=0, tiled=True),
        lax.all_to_all(value_send, "seq", split_axis=0, concat_axis=0, tiled=True),
    )
    my_table = lax.dynamic_index_in_dim(request_table, my_shard, 0, keepdims=False)
    my_owner = my_table // blocks_here
    by_owner = (my_owner[:, None] == jnp.arange(shards, dtype=jnp.int32)[None, :]).astype(jnp.int32)
    my_slot = jnp.sum((jnp.cumsum(by_owner, axis=0) - by_owner) * by_owner, axis=1)
    rand_shape = (heads_here, blocks_here, RAND_BLOCKS, BLOCK, HEAD_DIM)
    rand_keys = key_recv[my_owner, my_slot].reshape(rand_shape)
    rand_values = value_recv[my_owner, my_slot].reshape(rand_shape)
    attention_logits = (
        jnp.concatenate(
            [
                product("iahd,ijbhd->hiajb", query_tiles, window[0]),
                product("iahd,jbhd->hiajb", query_tiles, global_pair[0]),
                product("iahd,hijbd->hiajb", query_tiles, rand_keys),
            ],
            axis=3,
        )
        * score_scale
    )
    key_valid = jnp.concatenate(
        [window_ok, jnp.ones((blocks_here, GLOB_BLOCKS + RAND_BLOCKS), bool)], axis=1
    )
    attention_logits = jnp.where(key_valid[None, :, None, :, None], attention_logits, -jnp.inf)
    row_max = jnp.max(attention_logits, axis=(3, 4), keepdims=True)
    exponent = jnp.exp(attention_logits - row_max)
    row_sum = jnp.sum(exponent, axis=(3, 4), keepdims=True)
    probability = exponent / row_sum
    attention_weight = probability.astype(jnp.bfloat16)
    split_at = 3 + GLOB_BLOCKS
    weight_win = attention_weight[:, :, :, :3]
    weight_glob = attention_weight[:, :, :, 3:split_at]
    weight_rand = attention_weight[:, :, :, split_at:]
    mixed = product("hiajb,ijbhd->iahd", weight_win, window[1])
    mixed = mixed + product("hiajb,jbhd->iahd", weight_glob, global_pair[1])
    mixed = mixed + product("hiajb,hijbd->iahd", weight_rand, rand_values)
    attended = mixed.astype(jnp.bfloat16)
    out_rows = attended.reshape(tokens_here, width_here)
    row_delta = jnp.sum(
        incoming_gradient.astype(jnp.float32) * attended.astype(jnp.float32), axis=3
    ).transpose(2, 0, 1)[:, :, :, None, None]
    probability_gradient = jnp.concatenate(
        [
            product("iahd,ijbhd->hiajb", incoming_gradient, window[1]),
            product("iahd,jbhd->hiajb", incoming_gradient, global_pair[1]),
            product("iahd,hijbd->hiajb", incoming_gradient, rand_values),
        ],
        axis=3,
    )
    logit_gradient = (probability * (probability_gradient - row_delta)).astype(jnp.bfloat16)
    grad_win = logit_gradient[:, :, :, :3]
    grad_glob = logit_gradient[:, :, :, 3:split_at]
    grad_rand = logit_gradient[:, :, :, split_at:]
    query_gradient = product("hiajb,ijbhd->iahd", grad_win, window[0])
    query_gradient = query_gradient + product("hiajb,jbhd->iahd", grad_glob, global_pair[0])
    query_gradient = query_gradient + product("hiajb,hijbd->iahd", grad_rand, rand_keys)
    query_gradient = (
        (score_scale * query_gradient).astype(jnp.bfloat16).reshape(tokens_here, width_here)
    )
    near_grads = jnp.stack(
        [
            score_scale * product("hiajb,iahd->ijbhd", grad_win, query_tiles),
            product("hiajb,iahd->ijbhd", weight_win, incoming_gradient),
        ]
    )
    accum = (
        spread(near_grads[:, :, 1], 1)
        + spread(near_grads[:, :, 0], 0)
        + spread(near_grads[:, :, 2], 2)
    )
    rim_rows = jnp.concatenate([accum[:, :1], accum[:, -1:]], axis=1).reshape(
        2, 2 * BLOCK, width_here
    )
    arrived = extended(rim_rows.astype(jnp.bfloat16), (("seq", 1),), BLOCK).astype(rim_rows.dtype)
    arrived = arrived.reshape(2, 4, BLOCK, heads_here, HEAD_DIM)
    own_blocks = accum[:, 1:-1]
    own_blocks = own_blocks.at[:, 0].add(arrived[:, 0]).at[:, -1].add(arrived[:, 3])
    far_keys = score_scale * product("hiajb,iahd->jbhd", grad_glob, query_tiles)
    far_values = product("hiajb,iahd->jbhd", weight_glob, incoming_gradient)
    sum_keys, sum_values = lax.psum((far_keys, far_values), "seq")
    for glob_index in range(GLOB_BLOCKS):
        target = global_blocks[glob_index]
        owner_flag = (target // blocks_here == my_shard).astype(jnp.float32)
        addition = jnp.stack([sum_keys[glob_index], sum_values[glob_index]]) * owner_flag
        own_blocks = own_blocks.at[:, target % blocks_here].add(addition)
    tile_zero = jnp.zeros((shards, slot_count, BLOCK, HEAD_DIM), jnp.bfloat16)
    rand_grad_keys = (
        (score_scale * product("hiajb,iahd->hijbd", grad_rand, query_tiles))
        .astype(jnp.bfloat16)
        .reshape(requests, BLOCK, HEAD_DIM)
    )
    rand_grad_values = (
        product("hiajb,iahd->hijbd", weight_rand, incoming_gradient)
        .astype(jnp.bfloat16)
        .reshape(requests, BLOCK, HEAD_DIM)
    )
    keys_box = tile_zero.at[my_owner, my_slot].set(rand_grad_keys)
    values_box = tile_zero.at[my_owner, my_slot].set(rand_grad_values)
    back_keys, back_values = (
        lax.all_to_all(keys_box, "seq", split_axis=0, concat_axis=0, tiled=True),
        lax.all_to_all(values_box, "seq", split_axis=0, concat_axis=0, tiled=True),
    )
    selector = (
        (
            send_ids[:, :, None]
            == jnp.arange(heads_here * blocks_here, dtype=jnp.int32)[None, None, :]
        )
        & slot_used[:, :, None]
    ).astype(jnp.bfloat16)

    def collect(returned):
        summed = product("ncs,ncbd->sbd", selector, returned)
        return summed.reshape(heads_here, blocks_here, BLOCK, HEAD_DIM).transpose(1, 2, 0, 3)

    grad_key = (
        (own_blocks[0] + collect(back_keys)).astype(jnp.bfloat16).reshape(tokens_here, width_here)
    )
    grad_value = (
        (own_blocks[1] + collect(back_values)).astype(jnp.bfloat16).reshape(tokens_here, width_here)
    )
    return (
        lax.all_to_all(out_rows, "head", split_axis=0, concat_axis=1, tiled=True),
        lax.all_to_all(query_gradient, "head", split_axis=0, concat_axis=1, tiled=True),
        lax.all_to_all(grad_key, "head", split_axis=0, concat_axis=1, tiled=True),
        lax.all_to_all(grad_value, "head", split_axis=0, concat_axis=1, tiled=True),
    )


def solution(mesh):
    placed = (
        P(("seq", "head"), None),
        P(("seq", "head"), None),
        P(("seq", "head"), None),
        P(("seq", "head"), None),
        P(),
        P(),
    )
    return jax.shard_map(
        body,
        mesh=mesh,
        in_specs=placed,
        out_specs=(
            P(("seq", "head"), None),
            P(("seq", "head"), None),
            P(("seq", "head"), None),
            P(("seq", "head"), None),
        ),
        check_vma=False,
    )
```

profile of v0, /device:TPU:1, one launch (start us, length us, event | category | flops | bytes accessed | tf_op | source)
XLA Modules:
  0.0 674.4 jit_solution(14771707569633310795)
XLA Ops:
  7.2 1.7 copy.551
  8.9 5.0 all-to-all-start.1
  14.5 1.7 copy.552
  16.2 3.3 all-to-all-done.1
  19.5 3.4 all-to-all-start
  24.1 4.3 all-to-all-done
  28.4 4.0 all-to-all-start.6
  35.6 2.3 gather_fusion
  38.0 4.0 all-to-all-start.2
  42.0 3.9 broadcast_select_fusion
  48.3 16.4 %all-to-all-start.3 = ((bf16[64,2,64,128]{3,2,1,0:T(8,128)(2,1)}), bf16[64,2,64,128]{3,2,1,0:T(8,128)(2,1)S(1)}, u32[]{:S(2)}, u32[]{:S(2)}) async-start(bf16[64,2,64,128]{3,2,1,0:T(8,128)(2,1)} %get-tuple-element.91), calls=%async_computation.3 | async-start | bytes 4194304 | tf_op jit(solution)/shard_map/all_to_all | solution.py:97
  73.0 2.4 collective-permute-start.1
  75.4 3.2 collective-permute-start
  79.4 37.0 %all-to-all-done.3 = bf16[64,2,64,128]{3,2,1,0:T(8,128)(2,1)S(1)} async-done(((bf16[64,2,64,128]{3,2,1,0:T(8,128)(2,1)}), bf16[64,2,64,128]{3,2,1,0:T(8,128)(2,1)S(1)}, u32[]{:S(2)}, u32[]{:S(2)}) %all-to-all-start.3) | async-done | bytes 2097184 | tf_op jit(solution)/shard_map/all_to_all | solution.py:97
  117.7 5.2 all-to-all-start.4
  124.0 1.9 dynamic-slice_select_fusion
  129.3 184.8 %all-reduce.10.cloned.1.call-done = (bf16[2,1,64,8,128]{4,2,1,3,0:T(8,128)(2,1)}, bf16[2,1,64,8,128]{4,2,1,3,0:T(8,128)(2,1)}) async-done(((bf16[2,1,64,8,128]{4,2,1,3,0:T(8,128)(2,1)}, bf16[2,1,64,8,128]{4,2,1,3,0:T(8,128)(2,1)}), (bf16[2,1,64,8,128]{4,2,1,3,0:T(8,128)(2,1)}, bf16[2,1,64,8,128]{4,2,1,3,0:T(8,128)(2,1)})) %all-reduce.10.cloned.1.call-update) | async-done | bytes 524304 | tf_op jit(solution)/shard_map/psum | solution.py:27
  318.9 3.4 gather_fusion.1
  329.8 1.9 broadcast_in_dim.44.clone
  331.6 7.5 %scatter_fusion.1 = bf16[64,2,64,128]{3,2,1,0:T(8,128)(2,1)} fusion(bf16[64,2,64,128]{3,2,1,0:T(8,128)(2,1)} %broadcast_in_dim.44.clone, s32[48]{0:T(128)S(1)} %get-tuple-element.92, bf16[48,64,128]{2,1,0:T(8,128)(2,1)} %bitcast.339), kind=kCustom, calls=%fused_computation.5 | custom fusion | bytes 2359680 | tf_op jit(solution)/shard_map/scatter | solution.py:195
  339.1 5.1 copy.382
  344.2 9.1 %all-to-all-start.10 = ((bf16[64,2,64,128]{3,1,2,0:T(2,128)(2,1)}), bf16[64,2,64,128]{3,1,2,0:T(2,128)(2,1)}, u32[]{:S(2)}, u32[]{:S(2)}) async-start(bf16[64,2,64,128]{3,1,2,0:T(2,128)(2,1)} %copy.382), calls=%async_computation.10 | async-start | bytes 4194304 | tf_op jit(solution)/shard_map/all_to_all | solution.py:198
  354.2 2.5 convolution_bitcast_fusion.5
  359.4 3.4 gather_fusion.3
  365.9 2.2 multiply_reduce_fusion
  368.6 1.7 fusion.2
  371.9 1.8 broadcast_in_dim.44.clone.1
  373.7 6.8 %scatter_fusion = bf16[64,2,64,128]{3,2,1,0:T(8,128)(2,1)} fusion(bf16[64,2,64,128]{3,2,1,0:T(8,128)(2,1)} %broadcast_in_dim.44.clone.1, s32[48]{0:T(128)S(1)} %get-tuple-element.92, bf16[48,64,128]{2,1,0:T(8,128)(2,1)S(1)} %bitcast.338), kind=kCustom, calls=%fused_computation.4 | custom fusion | bytes 2359680 | tf_op jit(solution)/shard_map/scatter | solution.py:194
  380.5 5.3 copy.375
  388.3 14.6 %all-to-all-done.10 = bf16[64,2,64,128]{3,1,2,0:T(2,128)(2,1)} async-done(((bf16[64,2,64,128]{3,1,2,0:T(2,128)(2,1)}), bf16[64,2,64,128]{3,1,2,0:T(2,128)(2,1)}, u32[]{:S(2)}, u32[]{:S(2)}) %all-to-all-start.10) | async-done | bytes 2097184 | tf_op jit(solution)/shard_map/all_to_all | solution.py:198
  402.9 7.2 %all-to-all-start.8 = ((bf16[64,2,64,128]{3,1,2,0:T(2,128)(2,1)}), bf16[64,2,64,128]{3,1,2,0:T(2,128)(2,1)}, u32[]{:S(2)}, u32[]{:S(2)}) async-start(bf16[64,2,64,128]{3,1,2,0:T(2,128)(2,1)} %copy.375), calls=%async_computation.8 | async-start | bytes 4194304 | tf_op jit(solution)/shard_map/all_to_all | solution.py:197
  412.2 1.8 fusion.95
  415.3 2.1 convert_element_type.79
  417.3 2.0 fusion.102
  419.3 2.4 collective-permute-start.3
  421.7 3.4 collective-permute-start.2
  427.8 2.1 convolution_bitcast_fusion.7
  437.7 185.3 %all-reduce.8.cloned.1.call-done = (f32[2,64,8,128]{3,1,2,0:T(8,128)}, f32[2,64,8,128]{3,1,2,0:T(8,128)}) async-done(((f32[2,64,8,128]{3,1,2,0:T(8,128)}, f32[2,64,8,128]{3,1,2,0:T(8,128)}), (f32[2,64,8,128]{3,1,2,0:T(8,128)}, f32[2,64,8,128]{3,1,2,0:T(8,128)})) %all-reduce.8.cloned.1.call-update) | async-done | bytes 1048592 | tf_op jit(solution)/shard_map/psum | solution.py:177
  626.7 3.9 fusion.5
  630.6 4.0 all-to-all-start.5
  634.6 3.9 fusion.7
  638.5 1.6 all-to-all-done.5
  640.1 3.4 all-to-all-start.7
  644.9 4.1 all-to-all-done.7
  649.0 3.4 all-to-all-start.9
  653.4 4.5 all-to-all-done.9
  657.9 3.4 all-to-all-start.11
  663.5 3.3 all-to-all-done.11
  (194 shorter events, 62.6 us)
Async XLA Ops:
  7.2 6.8 %copy-start = (s32[32,128,3]{1,0,2:T(8,128)S(1)}, s32[32,128,3]{1,0,2:T(8,128)}, u32[]{:S(2)}) copy-start(s32[32,128,3]{1,0,2:T(8,128)} %param.18) | copy-start | bytes 147460
  7.2 15.8 %copy-start.36 = (bf16[32,4096]{1,0:T(8,128)(2,1)S(1)}, bf16[32,4096]{1,0:T(8,128)(2,1)}, u32[]{:S(2)}) copy-start(bf16[32,4096]{1,0:T(8,128)(2,1)} %param.17) | copy-start | bytes 786436
  7.2 25.7 %copy-start.37 = (bf16[32,4096]{1,0:T(8,128)(2,1)S(1)}, bf16[32,4096]{1,0:T(8,128)(2,1)}, u32[]{:S(2)}) copy-start(bf16[32,4096]{1,0:T(8,128)(2,1)} %param.14) | copy-start | bytes 786436
  8.9 10.5 %all-to-all-start.1 = ((bf16[32,4,1024]{2,0,1:T(8,128)(2,1)}), bf16[32,4,1024]{2,0,1:T(8,128)(2,1)S(1)}, u32[]{:S(2)}, u32[]{:S(2)}) async-start(bf16[32,4,1024]{2,0,1:T(8,128)(2,1)} %bitcast.318), calls=%async_computation.1 | async-start | bytes 524288 | tf_op jit(solution)/shard_map/all_to_all | solution.py:44
  19.5 8.9 %all-to-all-start = ((bf16[32,4,1024]{2,0,1:T(8,128)(2,1)}), bf16[32,4,1024]{2,0,1:T(8,128)(2,1)S(1)}, u32[]{:S(2)}, u32[]{:S(2)}) async-start(bf16[32,4,1024]{2,0,1:T(8,128)(2,1)} %bitcast.319), calls=%async_computation | async-start | bytes 524288 | tf_op jit(solution)/shard_map/all_to_all | solution.py:43
  28.4 9.6 %all-to-all-start.6 = ((bf16[32,4,1024]{2,0,1:T(8,128)(2,1)}), bf16[32,4,1024]{2,0,1:T(8,128)(2,1)}, u32[]{:S(2)}, u32[]{:S(2)}) async-start(bf16[32,4,1024]{2,0,1:T(8,128)(2,1)} %bitcast.316), calls=%async_computation.6 | async-start | bytes 524288 | tf_op jit(solution)/shard_map/all_to_all | solution.py:45
  38.0 9.5 %all-to-all-start.2 = ((bf16[32,4,1024]{2,0,1:T(8,128)(2,1)}), bf16[32,4,1024]{2,0,1:T(8,128)(2,1)S(1)}, u32[]{:S(2)}, u32[]{:S(2)}) async-start(bf16[32,4,1024]{2,0,1:T(8,128)(2,1)} %bitcast.355), calls=%async_computation.2 | async-start | bytes 524288 | tf_op jit(solution)/shard_map/all_to_all | solution.py:42
  47.6 17.2 %copy-start.38 = (s32[2]{0:T(128)S(1)}, s32[2]{0:T(128)}, u32[]{:S(2)}) copy-start(s32[2]{0:T(128)} %param.19) | copy-start | bytes 28
  48.3 68.1 %all-to-all-start.3 = ((bf16[64,2,64,128]{3,2,1,0:T(8,128)(2,1)}), bf16[64,2,64,128]{3,2,1,0:T(8,128)(2,1)S(1)}, u32[]{:S(2)}, u32[]{:S(2)}) async-start(bf16[64,2,64,128]{3,2,1,0:T(8,128)(2,1)} %get-tuple-element.91), calls=%async_computation.3 | async-start | bytes 4194304 | tf_op jit(solution)/shard_map/all_to_all | solution.py:97
  64.7 13.9 %copy-start.31 = (bf16[16,8,8,128]{3,2,1,0:T(8,128)(2,1)S(1)}, bf16[16,8,8,128]{3,2,1,0:T(8,128)(2,1)}, u32[]{:S(2)}) copy-start(bf16[16,8,8,128]{3,2,1,0:T(8,128)(2,1)} %copy-done.30) | copy-start | bytes 786436
  72.1 6.5 copy-start.33
  73.0 54.6 %collective-permute-start.1 = (bf16[2,64,1024]{2,1,0:T(8,128)(2,1)}, bf16[2,64,1024]{2,1,0:T(8,128)(2,1)}, u32[]{:S(2)}, u32[]{:S(2)}) collective-permute-start(bf16[2,64,1024]{2,1,0:T(8,128)(2,1)} %get-tuple-element.87), channel_id=1, source_target_pairs={{4,0},{8,4},{12,8},{16,12},{20,16},{24,20},{28,24},{32,28},{36,32}... | collective-permute-start | bytes 786440 | tf_op jit(solution)/shard_map/ppermute | solution.py:20
  75.4 52.2 %collective-permute-start = (bf16[2,64,1024]{2,1,0:T(8,128)(2,1)}, bf16[2,64,1024]{2,1,0:T(8,128)(2,1)}, u32[]{:S(2)}, u32[]{:S(2)}) collective-permute-start(bf16[2,64,1024]{2,1,0:T(8,128)(2,1)} %get-tuple-element.86), channel_id=1, source_target_pairs={{0,4},{4,8},{8,12},{12,16},{16,20},{20,24},{24,28},{28,32},{32,36}... | collective-permute-start | bytes 786440 | tf_op jit(solution)/shard_map/ppermute | solution.py:19
  117.7 226.5 %all-to-all-start.4 = ((bf16[64,2,64,128]{3,2,1,0:T(8,128)(2,1)}), bf16[64,2,64,128]{3,2,1,0:T(8,128)(2,1)}, u32[]{:S(2)}, u32[]{:S(2)}) async-start(bf16[64,2,64,128]{3,2,1,0:T(8,128)(2,1)} %get-tuple-element.90), calls=%async_computation.4 | async-start | bytes 4194304 | tf_op jit(solution)/shard_map/all_to_all | solution.py:98
  123.0 191.2 %all-reduce.10.cloned.1.call-start = ((), (), s32[]{:S(2)}) async-start(), calls=%async_computation.13 | async-start | bytes 1048576 | tf_op jit(solution)/shard_map/psum | solution.py:27
  126.8 2.2 copy-start.27
  317.0 1.6 copy-start.4
  322.3 1.6 copy-start.2
  325.9 2.6 copy-start.9
  344.2 9.3 %copy-start.39 = (s32[5]{0:T(128)S(1)}, s32[5]{0:T(128)}, u32[]{:S(2)}) copy-start(s32[5]{0:T(128)} %constant.247.clone.1) | copy-start | bytes 64
  344.2 58.7 %all-to-all-start.10 = ((bf16[64,2,64,128]{3,1,2,0:T(2,128)(2,1)}), bf16[64,2,64,128]{3,1,2,0:T(2,128)(2,1)}, u32[]{:S(2)}, u32[]{:S(2)}) async-start(bf16[64,2,64,128]{3,1,2,0:T(2,128)(2,1)} %copy.382), calls=%async_computation.10 | async-start | bytes 4194304 | tf_op jit(solution)/shard_map/all_to_all | solution.py:198
  353.5 3.1 copy-start.5
  354.2 3.8 copy-start.10
  362.8 1.7 copy-start.17
  362.8 2.1 copy-start.26
  365.0 3.2 copy-start.11
  365.9 2.6 copy-start.3
  365.9 2.6 copy-start.18
  365.9 2.6 copy-start.20
  380.5 5.3 copy-start.8
  386.8 16.1 %copy-start.14 = (bf16[8,2,64,3,64]{2,4,3,1,0:T(8,128)(2,1)}, bf16[8,2,64,3,64]{2,4,3,1,0:T(8,128)(2,1)S(1)}, u32[]{:S(2)}) copy-start(bf16[8,2,64,3,64]{2,4,3,1,0:T(8,128)(2,1)S(1)} %get-tuple-element.67) | copy-start | bytes 1179652
  388.3 21.8 %copy-start.12 = (bf16[2,64,8,128,1]{3,2,1,0,4:T(8,128)(2,1)S(1)}, bf16[2,64,8,128,1]{3,2,1,0,4:T(8,128)(2,1)}, u32[]{:S(2)}) copy-start(bf16[2,64,8,128,1]{3,2,1,0,4:T(8,128)(2,1)} %bitcast_bitcast_fusion) | copy-start | bytes 786436
  402.9 227.7 %all-to-all-start.8 = ((bf16[64,2,64,128]{3,1,2,0:T(2,128)(2,1)}), bf16[64,2,64,128]{3,1,2,0:T(2,128)(2,1)}, u32[]{:S(2)}, u32[]{:S(2)}) async-start(bf16[64,2,64,128]{3,1,2,0:T(2,128)(2,1)} %copy.375), calls=%async_computation.8 | async-start | bytes 4194304 | tf_op jit(solution)/shard_map/all_to_all | solution.py:197
  410.1 212.9 %all-reduce.8.cloned.1.call-start = ((), (), s32[]{:S(2)}) async-start(), calls=%async_computation.12 | async-start | bytes 2097152 | tf_op jit(solution)/shard_map/psum | solution.py:177
  410.2 1.6 copy-start.19
  414.1 11.1 %copy-start.13 = (bf16[48,64,128]{2,1,0:T(8,128)(2,1)S(1)}, bf16[48,64,128]{2,1,0:T(8,128)(2,1)}, u32[]{:S(2)}) copy-start(bf16[48,64,128]{2,1,0:T(8,128)(2,1)} %gather_fusion.1) | copy-start | bytes 2359300
  417.3 9.4 %copy-start.15 = (bf16[8,2,64,3,64]{2,4,3,1,0:T(8,128)(2,1)S(1)}, bf16[8,2,64,3,64]{2,4,3,1,0:T(8,128)(2,1)}, u32[]{:S(2)}) copy-start(bf16[8,2,64,3,64]{2,4,3,1,0:T(8,128)(2,1)} %copy-done.14) | copy-start | bytes 1179652
  417.3 9.5 %copy-start.25 = (bf16[2,3,64,8,128]{4,2,1,0,3:T(8,128)(2,1)S(1)}, bf16[2,3,64,8,128]{4,2,1,0,3:T(8,128)(2,1)}, u32[]{:S(2)}) copy-start(bf16[2,3,64,8,128]{4,2,1,0,3:T(8,128)(2,1)} %get-tuple-element.71) | copy-start | bytes 2359300
  419.3 15.0 %collective-permute-start.3 = (bf16[2,64,1024]{2,1,0:T(8,128)(2,1)}, bf16[2,64,1024]{2,1,0:T(8,128)(2,1)}, u32[]{:S(2)}, u32[]{:S(2)}) collective-permute-start(bf16[2,64,1024]{2,1,0:T(8,128)(2,1)} %get-tuple-element.85), channel_id=1, source_target_pairs={{4,0},{8,4},{12,8},{16,12},{20,16},{24,20},{28,24},{32,28},{36,32}... | collective-permute-start | bytes 786440 | tf_op jit(solution)/shard_map/ppermute | solution.py:20
  421.7 12.6 %collective-permute-start.2 = (bf16[2,64,1024]{2,1,0:T(8,128)(2,1)}, bf16[2,64,1024]{2,1,0:T(8,128)(2,1)}, u32[]{:S(2)}, u32[]{:S(2)}) collective-permute-start(bf16[2,64,1024]{2,1,0:T(8,128)(2,1)} %get-tuple-element.84), channel_id=1, source_target_pairs={{0,4},{4,8},{8,12},{12,16},{16,20},{20,24},{24,28},{28,32},{32,36}... | collective-permute-start | bytes 786440 | tf_op jit(solution)/shard_map/ppermute | solution.py:19
  425.2 2.1 copy-start.24
  427.3 2.6 copy-start.32
  429.9 3.3 copy-start.34
  630.6 9.5 %all-to-all-start.5 = ((bf16[4,32,1024]{2,1,0:T(8,128)(2,1)}), bf16[4,32,1024]{2,1,0:T(8,128)(2,1)S(1)}, u32[]{:S(2)}, u32[]{:S(2)}) async-start(bf16[4,32,1024]{2,1,0:T(8,128)(2,1)} %all_to_all.127), calls=%async_computation.5 | async-start | bytes 524288 | tf_op jit(solution)/shard_map/all_to_all | solution.py:219
  640.1 8.9 %all-to-all-start.7 = ((bf16[4,32,1024]{2,1,0:T(8,128)(2,1)}), bf16[4,32,1024]{2,1,0:T(8,128)(2,1)S(1)}, u32[]{:S(2)}, u32[]{:S(2)}) async-start(bf16[4,32,1024]{2,1,0:T(8,128)(2,1)} %all_to_all.134), calls=%async_computation.7 | async-start | bytes 524288 | tf_op jit(solution)/shard_map/all_to_all | solution.py:220
  644.1 23.5 %copy-start.1 = (s32[32,128,3]{1,0,2:T(8,128)S(1)}, s32[32,128,3]{1,0,2:T(8,128)}, u32[]{:S(2)}) copy-start(s32[32,128,3]{1,0,2:T(8,128)} %param.18) | copy-start | bytes 147460
  649.0 8.9 %all-to-all-start.9 = ((bf16[4,32,1024]{2,1,0:T(8,128)(2,1)}), bf16[4,32,1024]{2,1,0:T(8,128)(2,1)S(1)}, u32[]{:S(2)}, u32[]{:S(2)}) async-start(bf16[4,32,1024]{2,1,0:T(8,128)(2,1)} %all_to_all.139), calls=%async_computation.9 | async-start | bytes 524288 | tf_op jit(solution)/shard_map/all_to_all | solution.py:221
  657.9 8.9 %all-to-all-start.11 = ((bf16[4,32,1024]{2,1,0:T(8,128)(2,1)}), bf16[4,32,1024]{2,1,0:T(8,128)(2,1)S(1)}, u32[]{:S(2)}, u32[]{:S(2)}) async-start(bf16[4,32,1024]{2,1,0:T(8,128)(2,1)} %all_to_all.144), calls=%async_computation.11 | async-start | bytes 524288 | tf_op jit(solution)/shard_map/all_to_all | solution.py:222
  (10 other events, 10.9 us)
Sparse Core Ops, SparseCore 0:
  127.9 186.2 all-reduce.9
  434.4 188.5 all-reduce.7
where the time goes:
time: 683 us; the launch traced here: 674 us
  waiting for transfers between devices  445 us (65%)
  starting transfers between devices  80.3 us (12%)
  local copies, waits for them, and re-layouts  78.9 us (12%)
  matrix products  29 us (4%)
  other arithmetic  21.3 us (3%)
  between operations  20.2 us (3%)
    psum x1, waiting for transfers between devices, body(): sum_keys, sum_values = lax.psum((far_keys, far_values), 'seq')  185 us
    psum x1, waiting for transfers between devices, spread_2(): return lax.psum(jnp.where(mine, shard, jnp.zeros_like(shard)), axis)  185 us
    all_to_all x1, waiting for transfers between devices, body(): lax.all_to_all(key_send, 'seq', split_axis=0, concat_axis=0, tiled=True)  37 us
    dot_general x20, matrix products, product(): jnp.einsum(formula, former, latter, preferred_element_type=jnp.float32)  29 us
    all_to_all x1, starting transfers between devices, body(): lax.all_to_all(key_send, 'seq', split_axis=0, concat_axis=0, tiled=True)  16.4 us
    all_to_all x1, waiting for transfers between devices, body(): lax.all_to_all(values_box, 'seq', split_axis=0, concat_axis=0, tiled=True)  14.6 us
  transfers between devices with their start and end apart: 18, of which 12 were waited for; matrix products, arithmetic and copies ran while one was open for 17% of the time, Pallas kernels for 0%

commit v1 on v0

v1 whole, which is shorter than its diff:
```python
import functools
import jax
import jax.numpy as jnp
from jax import lax
from jax.experimental import pallas as pl
from jax.experimental.pallas import tpu as pltpu
from jax.sharding import PartitionSpec as P

HEAD_DIM = 128
BLOCK = 64
SCALE = HEAD_DIM ** -0.5
BLOCKS = 128
LOCAL = 16
NT = (((1,), (1,)), ((), ()))
TN = (((0,), (0,)), ((), ()))


def dot(a, b, dims=(((1,), (0,)), ((), ()))):
    return lax.dot_general(a, b, dims, preferred_element_type=jnp.float32)


def attention_kernel(rand_ref, glob_ref, place_ref, qg_ref, kv_ref, out_ref, dkv_ref, acc):
    acc[...] = jnp.zeros_like(acc)
    place = place_ref[0]

    def one(local, carry):
        block = (local // 2) * 16 + place * 2 + local % 2
        names = [
            jnp.maximum(block - 1, 0),
            block,
            jnp.minimum(block + 1, BLOCKS - 1),
            glob_ref[0],
            glob_ref[1],
        ] + [rand_ref[block * 3 + r] for r in range(3)]
        starts = [pl.multiple_of(n * BLOCK, BLOCK) for n in names]
        rows = pl.ds(pl.multiple_of(local * BLOCK, BLOCK), BLOCK)
        q = qg_ref[0, rows, :]
        g = qg_ref[1, rows, :]
        k = jnp.concatenate([kv_ref[0, pl.ds(s, BLOCK), :] for s in starts], axis=0)
        v = jnp.concatenate([kv_ref[1, pl.ds(s, BLOCK), :] for s in starts], axis=0)
        lane = lax.broadcasted_iota(jnp.int32, (1, 8 * BLOCK), 1) // BLOCK
        gone = ((lane == 0) & (block == 0)) | ((lane == 2) & (block == BLOCKS - 1))
        bias = jnp.where(gone, -jnp.inf, 0.0)
        s = dot(q, k, NT) * SCALE + bias
        dp = dot(g, v, NT)
        e = jnp.exp(s - jnp.max(s, axis=1, keepdims=True))
        p = e * (1.0 / jnp.sum(e, axis=1, keepdims=True))
        w = p.astype(jnp.bfloat16)
        o = dot(w, v).astype(jnp.bfloat16)
        delta = jnp.sum(g.astype(jnp.float32) * o.astype(jnp.float32), axis=1, keepdims=True)
        ds = (p * (dp - delta)).astype(jnp.bfloat16)
        out_ref[0, rows, :] = o
        out_ref[1, rows, :] = (SCALE * dot(ds, k)).astype(jnp.bfloat16)
        dk = dot(ds, q, TN)
        dv = dot(w, g, TN)
        for n, st in enumerate(starts):
            acc[0, pl.ds(st, BLOCK), :] += dk[n * BLOCK:(n + 1) * BLOCK]
            acc[1, pl.ds(st, BLOCK), :] += dv[n * BLOCK:(n + 1) * BLOCK]
        return carry

    lax.fori_loop(0, LOCAL, one, 0)

    def finish(t, carry):
        rows = pl.ds(pl.multiple_of(t * 256, 256), 256)
        dkv_ref[0, rows, :] = (SCALE * acc[0, rows, :]).astype(jnp.bfloat16)
        dkv_ref[1, rows, :] = acc[1, rows, :].astype(jnp.bfloat16)
        return carry

    lax.fori_loop(0, BLOCKS * BLOCK // 256, finish, 0)


def attention(rand, glob, place, qg, kv):
    vm = pl.BlockSpec(memory_space=pltpu.VMEM)
    sm = pl.BlockSpec(memory_space=pltpu.SMEM)
    return pl.pallas_call(
        attention_kernel,
        out_shape=(
            jax.ShapeDtypeStruct((2, LOCAL * BLOCK, HEAD_DIM), jnp.bfloat16),
            jax.ShapeDtypeStruct((2, BLOCKS * BLOCK, HEAD_DIM), jnp.bfloat16),
        ),
        in_specs=[sm, sm, sm, vm, vm],
        out_specs=(vm, vm),
        scratch_shapes=[pltpu.VMEM((2, BLOCKS * BLOCK, HEAD_DIM), jnp.float32)],
        compiler_params=pltpu.CompilerParams(vmem_limit_bytes=48 * 1024 * 1024),
    )(rand, glob, place, qg, kv)


def body(queries, keys, values, grad_out, random_blocks, global_blocks):
    z, x, c, y = (lax.axis_index(a) for a in ("z", "x", "core", "head"))
    rand = lax.dynamic_index_in_dim(random_blocks, z * 4 + y, 0, keepdims=False).reshape(-1)
    place = (x * 2 + c).reshape(1)
    stacked = jnp.stack([queries, grad_out, keys, values]).reshape(4, 32, 32, HEAD_DIM)
    got = lax.all_to_all(stacked, ("z", "head"), split_axis=2, concat_axis=1, tiled=False)
    qg = got[:2].reshape(2, LOCAL * BLOCK, HEAD_DIM)
    kv = lax.all_gather(got[2:], ("x", "core"), axis=0)
    kv = kv.reshape(8, 2, 8, 128, HEAD_DIM).transpose(1, 2, 0, 3, 4).reshape(2, BLOCKS * BLOCK, HEAD_DIM)
    out, dkv = attention(rand, global_blocks, place, qg, kv)
    dkv = dkv.reshape(2, 8, 8, 128, HEAD_DIM).transpose(2, 0, 1, 3, 4)
    dkv = lax.all_to_all(dkv, ("x", "core"), split_axis=0, concat_axis=0, tiled=True)
    dkv = jnp.sum(dkv.astype(jnp.float32), axis=0).astype(jnp.bfloat16)
    both = jnp.concatenate([out.reshape(2, 32, 32, HEAD_DIM), dkv.reshape(2, 32, 32, HEAD_DIM)])
    back = lax.all_to_all(both, ("z", "head"), split_axis=1, concat_axis=2, tiled=False)
    back = back.reshape(4, 32, 32 * HEAD_DIM)
    return back[0], back[1], back[2], back[3]


def solution(mesh):
    fine = jax.sharding.Mesh(mesh.devices.reshape(8, 4, 2, 4), ("z", "x", "core", "head"))
    rows = P(("z", "x", "core", "head"), None)
    return jax.shard_map(
        body,
        mesh=fine,
        in_specs=(rows, rows, rows, rows, P(), P()),
        out_specs=(rows, rows, rows, rows),
        check_vma=False,
    )
```

time: 683 us -> 210 us (0.31)
  waiting for transfers between devices: 445 us -> 34 us
  blocking collectives: 0 us -> 126 us
  starting transfers between devices: 80.3 us -> 0.04 us
  local copies, waits for them, and re-layouts: 78.9 us -> 13.6 us
  matrix products: 29 us -> 0 us
  other arithmetic: 21.3 us -> 3.18 us
  Pallas kernels: 0 us -> 16.4 us
    psum x2 -> x0, waiting for transfers between devices: 370 us -> none  [the longest x1 185 us: body(): sum_keys, sum_values = lax.psum((far_keys, far_values), 'seq')]
    all_to_all x0 -> x3, blocking collectives: none -> 126 us  [the longest x1 52.8 us: body(): lax.all_to_all(dkv, ('x', 'core'), split_axis=0, concat_axis=0, tiled=True)]
    all_to_all x12 -> x0, waiting for transfers between devices: 74.5 us -> none  [the longest x1 37 us: body(): lax.all_to_all(key_send, 'seq', split_axis=0, concat_axis=0, tiled=True)]
    all_to_all x12 -> x0, starting transfers between devices: 68.7 us -> none  [the longest x1 16.4 us: body(): lax.all_to_all(key_send, 'seq', split_axis=0, concat_axis=0, tiled=True)]
    all_gather x0 -> x1, waiting for transfers between devices: none -> 34 us  [body(): kv = lax.all_gather(got[2:], ('x', 'core'), axis=0)]
    dot_general x20 -> x0, matrix products: 29 us -> none  [product(): jnp.einsum(formula, former, latter, preferred_element_type=jnp.float32)]
    scatter x4 -> x0, local copies, waits for them, and re-layouts: 24.7 us -> none  [the longest x2 12.6 us: body(): values_box = tile_zero.at[my_owner, my_slot].set(rand_grad_values)]
    pallas_call x0 -> x1, Pallas kernels: none -> 16.4 us  [attention(): pl.pallas_call(attention_kernel, out_shape=(jax.ShapeDtypeStruct((2, LOCA...]
  transfers between devices with their start and end apart: 18 -> 1, of which waited for: 12 -> 1; matrix products, arithmetic and copies ran while one was open for 17% -> 0% of each run, Pallas kernels for 0% -> 0%
where the time goes in v1:
time: 210 us; the launch traced here: 207 us
  blocking collectives  126 us (60%)
  waiting for transfers between devices  34 us (16%)
  Pallas kernels  16.4 us (8%)
  between operations  14.2 us (7%)
  local copies, waits for them, and re-layouts  13.6 us (6%)
  other arithmetic  3.18 us (2%)
    all_to_all x1, blocking collectives, body(): lax.all_to_all(dkv, ('x', 'core'), split_axis=0, concat_axis=0, tiled=True)  52.8 us
    all_to_all x1, blocking collectives, body(): lax.all_to_all(stacked, ('z', 'head'), split_axis=2, concat_axis=1, tiled...  38 us
    all_to_all x1, blocking collectives, body(): lax.all_to_all(both, ('z', 'head'), split_axis=1, concat_axis=2, tiled=Fa...  35.2 us
    all_gather x1, waiting for transfers between devices, body(): kv = lax.all_gather(got[2:], ('x', 'core'), axis=0)  34 us
    pallas_call x1, Pallas kernels, attention(): pl.pallas_call(attention_kernel, out_shape=(jax.ShapeDtypeStruct((2, LOCA...  16.4 us
    transpose x1, local copies, waits for them, and re-layouts, body(): kv.reshape(8, 2, 8, 128, HEAD_DIM).transpose(1, 2, 0, 3, 4)  4.77 us
  transfers between devices with their start and end apart: 1, of which 1 were waited for; matrix products, arithmetic and copies ran while one was open for 0% of the time, Pallas kernels for 0%

profile of v1, /device:TPU:1, one launch (start us, length us, event | category | flops | bytes accessed | tf_op | source)
XLA Modules:
  0.0 207.5 jit_solution(13844740063896816809)
XLA Ops:
  7.2 0.0 copy-start
  7.2 0.0 all-gather.3.cloned.1.call-start
  7.2 1.0 copy.50
  8.2 1.0 copy.52
  9.2 1.0 copy.53
  10.2 1.0 copy.51
  11.2 0.1 pad_maximum_fusion
  11.4 0.4 copy.40
  11.8 38.0 %all_to_all.35 = bf16[4,1,32,32,128]{4,2,1,0,3:T(8,128)(2,1)S(1)} all-to-all(bf16[4,1,32,32,128]{4,2,1,0,3:T(8,128)(2,1)S(1)} %copy.40), channel_id=1, replica_groups=mesh['z'=8,'x'=4,'core'=2,'head'=4] {'z','head'}, dimensions={3} | all-to-all | bytes 2097152 | tf_op jit(solution)/shard_map/all_to_all | solution.py:93
  49.8 0.1 fusion.1
  49.9 0.8 copy.42
  50.7 0.0 all-gather.3.cloned.1.call-update
  50.8 0.0 copy-done
  50.8 0.1 copy.39
  50.9 0.2 reshape.55.rand_ref
  51.2 34.0 %all-gather.3.cloned.1.call-done = bf16[16,32,1,32,1,128]{5,3,4,2,1,0:T(8,128)(2,1)} async-done(((bf16[2,32,1,32,1,128]{5,3,4,2,1,0:T(8,128)(2,1)}), bf16[16,32,1,32,1,128]{5,3,4,2,1,0:T(8,128)(2,1)}) %all-gather.3.cloned.1.call-update) | async-done | bytes 4194320 | tf_op jit(solution)/shard_map/all_gather | solution.py:95
  85.2 0.0 copy-start.1
  85.2 4.8 %copy.43 = bf16[2,8,8,128,128]{4,3,2,1,0:T(8,128)(2,1)} copy(bf16[2,8,8,128,128]{4,3,1,0,2:T(8,128)(2,1)} %bitcast.57) | data formatting | bytes 8388608 | tf_op jit(solution)/shard_map/transpose | solution.py:96
  89.9 0.0 copy-done.1
  89.9 16.4 %shard_map.93 = (bf16[2,1024,128]{2,1,0:T(8,128)(2,1)S(1)}, bf16[2,8192,128]{2,1,0:T(8,128)(2,1)S(1)}) custom-call(s32[384]{0:T(512)S(1)} %reshape.55.rand_ref, s32[2]{0:T(128)S(1)} %copy-done.1, s32[1]{0:T(128)} %bitcast.place_ref, bf16[2,1024,128]{2,1,0:T(8,128)(2,1)S(1)} %bitcast.53, bf16[2,8192,128]{2,1,0:T(8,128)(2,1)} %bitcast.55), custom_call_target="tpu_custom_call" | custom-call | tf_op jit(solution)/shard_map/pallas_call | solution.py:75
  106.4 0.6 copy.63
  107.0 52.8 %all_to_all.36 = bf16[8,2,8,128,128]{4,3,2,1,0:T(8,128)(2,1)} all-to-all(bf16[8,2,8,128,128]{4,3,2,1,0:T(8,128)(2,1)S(1)} %bitcast.56), channel_id=1, replica_groups=mesh['z'=8,'x'=4,'core'=2,'head'=4] {'x','core'}, dimensions={0} | all-to-all | bytes 8388608 | tf_op jit(solution)/shard_map/all_to_all | solution.py:99
  159.8 2.9 %reduce_sum.12 = bf16[2,8,128,128]{3,2,1,0:T(8,128)(2,1)S(1)} reduce(bf16[8,2,8,128,128]{4,3,2,1,0:T(8,128)(2,1)} %all_to_all.36, bf16[]{:T(256)} %constant.29.clone.1), dimensions={0}, to_apply=%region_0.1 | reduce | flops 1835008 | bytes 4718594 | tf_op jit(solution)/shard_map/reduce_sum | solution.py:100
  162.7 0.1 maximum_bitcast_fusion
  162.8 0.1 copy.45
  163.0 35.2 %all_to_all.37 = bf16[4,32,32,1,128]{4,2,0,3,1:T(8,128)(2,1)S(1)} all-to-all(bf16[4,32,32,1,128]{4,2,0,3,1:T(8,128)(2,1)S(1)} %copy.45), channel_id=1, replica_groups=mesh['z'=8,'x'=4,'core'=2,'head'=4] {'z','head'}, dimensions={1} | all-to-all | bytes 2097152 | tf_op jit(solution)/shard_map/all_to_all | solution.py:102
  198.2 0.1 fusion
  198.3 0.1 copy.49
  198.4 0.1 copy.48
  198.5 0.1 copy.47
  198.6 0.1 copy.46
  198.7 1.0 copy_bitcast_fusion.1
  199.7 1.0 copy_bitcast_fusion.3
  (2 shorter events, 0.0 us)
Async XLA Ops:
  7.2 43.6 %copy-start = (s32[32,128,3]{1,0,2:T(8,128)S(1)}, s32[32,128,3]{1,0,2:T(8,128)}, u32[]{:S(2)}) copy-start(s32[32,128,3]{1,0,2:T(8,128)} %param.10) | copy-start | bytes 147460
  7.2 78.0 %all-gather.3.cloned.1.call-start = ((), (), s32[]{:S(2)}) async-start(), calls=%async_computation.3 | async-start | bytes 4718592 | tf_op jit(solution)/shard_map/all_gather | solution.py:95
  85.2 4.8 %copy-start.1 = (s32[2]{0:T(128)S(1)}, s32[2]{0:T(128)}, u32[]{:S(2)}) copy-start(s32[2]{0:T(128)} %glob_ref.1) | copy-start | bytes 28
Sparse Core Ops, SparseCore 0:
  50.9 34.2 all-gather.2

commit v2 on v1

--- a/solution.py
+++ b/solution.py
@@ -84,16 +84,140 @@
         compiler_params=pltpu.CompilerParams(vmem_limit_bytes=48 * 1024 * 1024),
     )(rand, glob, place, qg, kv)
 
+MESH = pl.DeviceIdType.MESH
+NZ, NX, NC, NY = 8, 4, 2, 4
+ROWS = 32
+WIDTH = 4096
+ORDER = (0, 1, 7, 2, 6, 3, 5, 4)
+
+
+def places():
+    return tuple(lax.axis_index(a) for a in ("z", "x", "core", "head"))
+
+
+def greet(z, x, c, y):
+    barrier = pltpu.get_barrier_semaphore()
+
+    def hello(zz, xx, cc, yy):
+        pl.semaphore_signal(barrier, inc=1, device_id=(zz, xx, cc, yy), device_id_type=MESH)
+
+    hello(z, x, 1 - c, y)
+    hello(z, (x + 1) % NX, c, y)
+    hello(z, (x + 3) % NX, c, y)
+
+    def one(i, carry):
+        hello((z + i // NY) % NZ, x, c, (y + i % NY) % NY)
+        return carry
+
+    lax.fori_loop(1, NZ * NY, one, 0)
+    pl.semaphore_wait(barrier, NZ * NY - 1 + 3)
+
+
+def drain(like, sem):
+    pltpu.make_async_copy(like, like, sem).wait()
+
+
+def gather_kernel(q_ref, g_ref, k_ref, v_ref, qg_ref, kv_ref, stage, stage_sem, out_sem, ring_out_sem,
+                  qg_sem, a_sem, l_sem, r_sem, f_sem, s_sem):
+    z, x, c, y = places()
+    loads = [
+        pltpu.make_async_copy(src, stage.at[n], stage_sem.at[n])
+        for n, src in ((2, k_ref), (3, v_ref), (0, q_ref), (1, g_ref))
+    ]
+    for load in loads:
+        load.start()
+    greet(z, x, c, y)
+    right, left, over = (x + 1) % NX, (x + 3) % NX, (x + 2) % NX
+
+    def columns(zz, yy):
+        return pl.ds(pl.multiple_of((zz * NY + yy) * HEAD_DIM, HEAD_DIM), HEAD_DIM)
+
+    mine = pl.ds(pl.multiple_of(y * ROWS, ROWS), ROWS)
+
+    def scatter(step, first, dst, sem):
+        zz = (z + ORDER[step]) % NZ
+
+        def one(i, carry):
+            yy = (y + i) % NY
+            pltpu.make_async_remote_copy(
+                src_ref=stage.at[pl.ds(first, 2), :, columns(zz, yy)], dst_ref=dst, send_sem=out_sem, recv_sem=sem,
+                device_id=(zz, x, c, yy), device_id_type=MESH,
+            ).start()
+            return carry
+
+        if ORDER[step] == 0:
+            pltpu.make_async_copy(stage.at[pl.ds(first, 2), :, columns(z, y)], dst, sem).start()
+        lax.fori_loop(1 if ORDER[step] == 0 else 0, NY, one, 0)
+
+    loads[0].wait()
+    loads[1].wait()
+    for step in range(NZ):
+        scatter(step, 2, kv_ref.at[:, z, x, c, mine, :], a_sem.at[z])
+    loads[2].wait()
+    loads[3].wait()
+
+    def send(zz, xx, to, sem):
+        part = kv_ref.at[:, zz, xx, c]
+        pltpu.make_async_remote_copy(
+            src_ref=part, dst_ref=part, send_sem=ring_out_sem, recv_sem=sem, device_id=to, device_id_type=MESH,
+        ).start()
+
+    to_right, to_left, to_twin = (z, right, c, y), (z, left, c, y), (z, x, 1 - c, y)
+    source = [(z + NZ - d) % NZ for d in ORDER]
+    for step in range(NZ + 2):
+        if step < NZ:
+            zz = source[step]
+            drain(kv_ref.at[:, zz, x, c], a_sem.at[zz])
+            send(zz, x, to_right, l_sem.at[zz])
+            send(zz, x, to_left, r_sem.at[zz])
+            send(zz, x, to_twin, s_sem)
+            scatter(step, 0, qg_ref.at[:, z, mine, :], qg_sem)
+        if 1 <= step < NZ + 1:
+            zz = source[step - 1]
+            drain(kv_ref.at[:, zz, left, c], l_sem.at[zz])
+            if step % 2 == 0:
+                send(zz, left, to_right, f_sem.at[zz])
+            send(zz, left, to_twin, s_sem)
+            drain(kv_ref.at[:, zz, right, c], r_sem.at[zz])
+            if step % 2 == 1:
+                send(zz, right, to_left, f_sem.at[zz])
+            send(zz, right, to_twin, s_sem)
+        if step >= 2:
+            zz = source[step - 2]
+            drain(kv_ref.at[:, zz, over, c], f_sem.at[zz])
+            send(zz, over, to_twin, s_sem)
+    drain(kv_ref.at[:, :, :, 1 - c], s_sem)
+    drain(qg_ref, qg_sem)
+    drain(stage.at[:, :, pl.ds(0, (NZ * NY - 1) * HEAD_DIM)], out_sem)
+    drain(kv_ref.at[:, pl.ds(0, NZ - 1)], ring_out_sem)
+
+
+def gather(q, g, k, v):
+    hbm = pl.BlockSpec(memory_space=pl.ANY)
+    dma = pltpu.SemaphoreType.DMA
+    return pl.pallas_call(
+        gather_kernel,
+        out_shape=(
+            jax.ShapeDtypeStruct((2, NZ, NY * ROWS, HEAD_DIM), jnp.bfloat16),
+            jax.ShapeDtypeStruct((2, NZ, NX, NC, NY * ROWS, HEAD_DIM), jnp.bfloat16),
+        ),
+        in_specs=[hbm] * 4,
+        out_specs=(hbm, hbm),
+        scratch_shapes=[
+            pltpu.VMEM((4, ROWS, WIDTH), jnp.bfloat16),
+            dma((4,)), dma, dma, dma, dma((NZ,)), dma((NZ,)), dma((NZ,)), dma((NZ,)), dma,
+        ],
+        compiler_params=pltpu.CompilerParams(collective_id=0, has_side_effects=True),
+    )(q, g, k, v)
+
 
 def body(queries, keys, values, grad_out, random_blocks, global_blocks):
-    z, x, c, y = (lax.axis_index(a) for a in ("z", "x", "core", "head"))
-    rand = lax.dynamic_index_in_dim(random_blocks, z * 4 + y, 0, keepdims=False).reshape(-1)
+    z, x, c, y = places()
+    rand = lax.dynamic_index_in_dim(random_blocks, z * NY + y, 0, keepdims=False).reshape(-1)
     place = (x * 2 + c).reshape(1)
-    stacked = jnp.stack([queries, grad_out, keys, values]).reshape(4, 32, 32, HEAD_DIM)
-    got = lax.all_to_all(stacked, ("z", "head"), split_axis=2, concat_axis=1, tiled=False)
-    qg = got[:2].reshape(2, LOCAL * BLOCK, HEAD_DIM)
-    kv = lax.all_gather(got[2:], ("x", "core"), axis=0)
-    kv = kv.reshape(8, 2, 8, 128, HEAD_DIM).transpose(1, 2, 0, 3, 4).reshape(2, BLOCKS * BLOCK, HEAD_DIM)
+    qg, kv = gather(queries, grad_out, keys, values)
+    qg = qg.reshape(2, LOCAL * BLOCK, HEAD_DIM)
+    kv = kv.reshape(2, BLOCKS * BLOCK, HEAD_DIM)
     out, dkv = attention(rand, global_blocks, place, qg, kv)
     dkv = dkv.reshape(2, 8, 8, 128, HEAD_DIM).transpose(2, 0, 1, 3, 4)
     dkv = lax.all_to_all(dkv, ("x", "core"), split_axis=0, concat_axis=0, tiled=True)
@@ -105,7 +229,7 @@
 
 
 def solution(mesh):
-    fine = jax.sharding.Mesh(mesh.devices.reshape(8, 4, 2, 4), ("z", "x", "core", "head"))
+    fine = jax.sharding.Mesh(mesh.devices.reshape(NZ, NX, NC, NY), ("z", "x", "core", "head"))
     rows = P(("z", "x", "core", "head"), None)
     return jax.shard_map(
         body,

time: 210 us -> 158 us (0.75)
  Pallas kernels: 16.4 us -> 61.2 us
  blocking collectives: 126 us -> 84.9 us
  waiting for transfers between devices: 34 us -> 0 us
  between operations: 14.2 us -> 0.75 us
  local copies, waits for them, and re-layouts: 13.6 us -> 5.92 us
    pallas_call x0 -> x1, Pallas kernels: none -> 44.7 us  [gather(): pl.pallas_call(gather_kernel, out_shape=(jax.ShapeDtypeStruct((2, NZ, NY...]
    all_to_all x1 -> x0, blocking collectives: 38 us -> none  [body(): lax.all_to_all(stacked, ('z', 'head'), split_axis=2, concat_axis=1, tiled...]
    all_gather x1 -> x0, waiting for transfers between devices: 34 us -> none  [body(): kv = lax.all_gather(got[2:], ('x', 'core'), axis=0)]
    transpose x1 -> x0, local copies, waits for them, and re-layouts: 4.77 us -> none  [body(): kv.reshape(8, 2, 8, 128, HEAD_DIM).transpose(1, 2, 0, 3, 4)]
    all_to_all x1, blocking collectives: 35.2 us -> 32 us  [body(): lax.all_to_all(both, ('z', 'head'), split_axis=1, concat_axis=2, tiled=Fa...]
  transfers between devices with their start and end apart: 1 -> 0, of which waited for: 1 -> 0; matrix products, arithmetic and copies ran while one was open for 0% -> 0% of each run, Pallas kernels for 0% -> 0%
where the time goes in v2:
time: 158 us; the launch traced here: 156 us
  blocking collectives  84.9 us (54%)
  Pallas kernels  61.2 us (39%)
  local copies, waits for them, and re-layouts  5.92 us (4%)
  other arithmetic  3.04 us (2%)
    all_to_all x1, blocking collectives, body(): lax.all_to_all(dkv, ('x', 'core'), split_axis=0, concat_axis=0, tiled=True)  52.9 us
    pallas_call x1, Pallas kernels, gather(): pl.pallas_call(gather_kernel, out_shape=(jax.ShapeDtypeStruct((2, NZ, NY...  44.7 us
    all_to_all x1, blocking collectives, body(): lax.all_to_all(both, ('z', 'head'), split_axis=1, concat_axis=2, tiled=Fa...  32 us
    pallas_call x1, Pallas kernels, attention(): pl.pallas_call(attention_kernel, out_shape=(jax.ShapeDtypeStruct((2, LOCA...  16.4 us

profile of v2, /device:TPU:1, one launch (start us, length us, event | category | flops | bytes accessed | tf_op | source)
XLA Modules:
  0.0 155.8 jit_solution(18305575848867822431)
XLA Ops:
  0.6 0.0 copy-start
  0.7 0.8 copy-done
  1.4 0.1 copy.22
  1.6 0.2 reshape.39.rand_ref
  1.8 44.7 %shard_map.93 = (bf16[2,8,128,128]{3,2,1,0:T(8,128)(2,1)}, bf16[2,8,4,2,128,128]{5,4,3,2,1,0:T(8,128)(2,1)}) custom-call(bf16[32,4096]{1,0:T(8,128)(2,1)} %q_ref.1, bf16[32,4096]{1,0:T(8,128)(2,1)} %g_ref.1, bf16[32,4096]{1,0:T(8,128)(2,1)} %k_ref.1, bf16[32,4096]{1,0:T(8,128)(2,1)} %v_ref.1), custom_call_target="tpu_custom_call" | custom-call | tf_op jit(solution)/shard_map/pallas_call | solution.py:198
  46.5 0.0 copy-start.1
  46.5 1.0 copy-done.1
  47.6 0.0 copy-start.2
  47.6 0.7 copy-done.2
  48.2 16.4 %shard_map.94 = (bf16[2,1024,128]{2,1,0:T(8,128)(2,1)S(1)}, bf16[2,8192,128]{2,1,0:T(8,128)(2,1)S(1)}) custom-call(s32[384]{0:T(512)S(1)} %reshape.39.rand_ref, s32[2]{0:T(128)S(1)} %copy-done.2, s32[1]{0:T(128)} %bitcast.place_ref, bf16[2,1024,128]{2,1,0:T(8,128)(2,1)S(1)} %bitcast.35, bf16[2,8192,128]{2,1,0:T(8,128)(2,1)} %bitcast.38), custom_call_target="tpu_custom_call" | custom-call | tf_op jit(solution)/shard_map/pallas_call | solution.py:75
  64.7 0.6 copy.38
  65.2 52.9 %all_to_all.20 = bf16[8,2,8,128,128]{4,3,2,1,0:T(8,128)(2,1)} all-to-all(bf16[8,2,8,128,128]{4,3,2,1,0:T(8,128)(2,1)S(1)} %bitcast.37), channel_id=1, replica_groups=mesh['z'=8,'x'=4,'core'=2,'head'=4] {'x','core'}, dimensions={0} | all-to-all | bytes 8388608 | tf_op jit(solution)/shard_map/all_to_all | solution.py:223
  118.2 2.9 %reduce_sum.12 = bf16[2,8,128,128]{3,2,1,0:T(8,128)(2,1)S(1)} reduce(bf16[8,2,8,128,128]{4,3,2,1,0:T(8,128)(2,1)} %all_to_all.20, bf16[]{:T(256)} %constant.29.clone.1), dimensions={0}, to_apply=%region_0.1 | reduce | flops 1835008 | bytes 4718594 | tf_op jit(solution)/shard_map/reduce_sum | solution.py:224
  121.1 0.1 maximum_bitcast_fusion
  121.2 0.1 copy.24
  121.3 32.0 %all_to_all.21 = bf16[4,32,32,1,128]{4,2,0,3,1:T(8,128)(2,1)S(1)} all-to-all(bf16[4,32,32,1,128]{4,2,0,3,1:T(8,128)(2,1)S(1)} %copy.24), channel_id=1, replica_groups=mesh['z'=8,'x'=4,'core'=2,'head'=4] {'z','head'}, dimensions={1} | all-to-all | bytes 2097152 | tf_op jit(solution)/shard_map/all_to_all | solution.py:226
  153.3 0.1 fusion
  153.4 0.1 copy.28
  153.5 0.1 copy.27
  153.6 0.1 copy.26
  153.7 0.1 copy.25
  153.9 1.0 copy_bitcast_fusion.1
  154.8 1.0 copy_bitcast_fusion.3
  (1 shorter events, 0.0 us)
Async XLA Ops:
  0.6 0.8 copy-start
  46.5 1.0 copy-start.1
  47.6 0.7 copy-start.2

commit v3 on v2

--- a/solution.py
+++ b/solution.py
@@ -211,6 +211,113 @@
     )(q, g, k, v)
 
 
+BACK = (4, 3, 5, 2, 6, 1, 7, 0)
+
+
+def return_kernel(od_ref, part_ref, od_out, kv_out, twin, sums, hop, joined, from_left, from_right, final,
+                  twin_out, ring_out, od_send, kv_send, twin_sem, hop_sem, l_sem, r_sem, od_sem, kv_sem):
+    z, x, c, y = places()
+    greet(z, x, c, y)
+    right, left, over = (x + 1) % NX, (x + 3) % NX, (x + 2) % NX
+    planes = [(z + d) % NZ for d in BACK]
+    columns = pl.ds(pl.multiple_of((z * NY + y) * HEAD_DIM, HEAD_DIM), HEAD_DIM)
+    for step in range(NZ):
+        pltpu.make_async_remote_copy(
+            src_ref=part_ref.at[:, planes[step], :, 1 - c], dst_ref=twin.at[step], send_sem=twin_out,
+            recv_sem=twin_sem.at[step], device_id=(z, x, 1 - c, y), device_id_type=MESH,
+        ).start()
+
+    def scatter(step, src, dst, send_sem, sem):
+        def rows(yy):
+            return src.at[:, pl.ds(pl.multiple_of(yy * ROWS, ROWS), ROWS), :]
+
+        def one(i, carry):
+            yy = (y + i) % NY
+            pltpu.make_async_remote_copy(
+                src_ref=rows(yy), dst_ref=dst.at[:, :, columns], send_sem=send_sem, recv_sem=sem,
+                device_id=(planes[step], x, c, yy), device_id_type=MESH,
+            ).start()
+            return carry
+
+        if BACK[step] == 0:
+            pltpu.make_async_copy(rows(y), dst.at[:, :, columns], sem).start()
+        lax.fori_loop(1 if BACK[step] == 0 else 0, NY, one, 0)
+
+    for step in range(NZ):
+        scatter(step, od_ref.at[:, planes[step]], od_out, od_send, od_sem)
+
+    def pass_on(src, dst, sem, xx):
+        pltpu.make_async_remote_copy(
+            src_ref=src, dst_ref=dst, send_sem=ring_out, recv_sem=sem, device_id=(z, xx, c, y), device_id_type=MESH,
+        ).start()
+
+    def wide(a):
+        return a.astype(jnp.float32)
+
+    for step in range(NZ + 2):
+        if step < NZ:
+            drain(twin.at[step], twin_sem.at[step])
+
+            def add(xx, carry, step=step):
+                for n in range(2):
+                    both = wide(part_ref[n, planes[step], xx, c]) + wide(twin[step, n, xx])
+                    sums[step, n, xx] = both.astype(jnp.bfloat16)
+                return carry
+
+            lax.fori_loop(0, NX, add, 0)
+            if step % 2 == 0:
+                pass_on(sums.at[step, :, over], hop.at[step], hop_sem.at[step], right)
+                pass_on(sums.at[step, :, left], from_right.at[step], r_sem.at[step], left)
+            else:
+                pass_on(sums.at[step, :, over], hop.at[step], hop_sem.at[step], left)
+                pass_on(sums.at[step, :, right], from_left.at[step], l_sem.at[step], right)
+        if 1 <= step < NZ + 1:
+            k = step - 1
+            drain(hop.at[k], hop_sem.at[k])
+            to = right if k % 2 == 0 else left
+            for n in range(2):
+                joined[k, n] = (wide(sums[k, n, to]) + wide(hop[k, n])).astype(jnp.bfloat16)
+            if k % 2 == 0:
+                pass_on(joined.at[k], from_left.at[k], l_sem.at[k], right)
+            else:
+                pass_on(joined.at[k], from_right.at[k], r_sem.at[k], left)
+        if step >= 2:
+            k = step - 2
+            drain(from_left.at[k], l_sem.at[k])
+            drain(from_right.at[k], r_sem.at[k])
+            for n in range(2):
+                total = wide(sums[k, n, x]) + wide(from_left[k, n]) + wide(from_right[k, n])
+                final[k, n] = total.astype(jnp.bfloat16)
+            scatter(k, final.at[k], kv_out, kv_send, kv_sem)
+    drain(part_ref.at[:, :, :, 0], twin_out)
+    drain(sums.at[:, :, pl.ds(0, NX - 1)], ring_out)
+    others = pl.ds(0, (NZ * NY - 1) * HEAD_DIM)
+    drain(od_out.at[:, :, others], od_send)
+    drain(kv_out.at[:, :, others], kv_send)
+    drain(od_out, od_sem)
+    drain(kv_out, kv_sem)
+
+
+def give_back(od, part):
+    hbm = pl.BlockSpec(memory_space=pl.ANY)
+    vm = pl.BlockSpec(memory_space=pltpu.VMEM)
+    dma = pltpu.SemaphoreType.DMA
+    rows = jax.ShapeDtypeStruct((2, ROWS, WIDTH), jnp.bfloat16)
+    chunk = pltpu.VMEM((NZ, 2, NY * ROWS, HEAD_DIM), jnp.bfloat16)
+    wide_chunk = pltpu.VMEM((NZ, 2, NX, NY * ROWS, HEAD_DIM), jnp.bfloat16)
+    each = dma((NZ,))
+    return pl.pallas_call(
+        return_kernel,
+        out_shape=(rows, rows),
+        in_specs=[vm, vm],
+        out_specs=(hbm, hbm),
+        scratch_shapes=[wide_chunk, wide_chunk] + [chunk] * 5 + [dma] * 4 + [each] * 4 + [dma, dma],
+        compiler_params=pltpu.CompilerParams(
+            collective_id=1, has_side_effects=True, vmem_limit_bytes=48 * 1024 * 1024
+        ),
+    )(od, part)
+
+
 def body(queries, keys, values, grad_out, random_blocks, global_blocks):
     z, x, c, y = places()
     rand = lax.dynamic_index_in_dim(random_blocks, z * NY + y, 0, keepdims=False).reshape(-1)
@@ -218,14 +325,11 @@
     qg, kv = gather(queries, grad_out, keys, values)
     qg = qg.reshape(2, LOCAL * BLOCK, HEAD_DIM)
     kv = kv.reshape(2, BLOCKS * BLOCK, HEAD_DIM)
-    out, dkv = attention(rand, global_blocks, place, qg, kv)
-    dkv = dkv.reshape(2, 8, 8, 128, HEAD_DIM).transpose(2, 0, 1, 3, 4)
-    dkv = lax.all_to_all(dkv, ("x", "core"), split_axis=0, concat_axis=0, tiled=True)
-    dkv = jnp.sum(dkv.astype(jnp.float32), axis=0).astype(jnp.bfloat16)
-    both = jnp.concatenate([out.reshape(2, 32, 32, HEAD_DIM), dkv.reshape(2, 32, 32, HEAD_DIM)])
-    back = lax.all_to_all(both, ("z", "head"), split_axis=1, concat_axis=2, tiled=False)
-    back = back.reshape(4, 32, 32 * HEAD_DIM)
-    return back[0], back[1], back[2], back[3]
+    od, part = attention(rand, global_blocks, place, qg, kv)
+    od, dkv = give_back(
+        od.reshape(2, NZ, NY * ROWS, HEAD_DIM), part.reshape(2, NZ, NX, NC, NY * ROWS, HEAD_DIM)
+    )
+    return od[0], od[1], dkv[0], dkv[1]
 
 
 def solution(mesh):

time: 158 us -> 100 us (0.63)
  the two profiles are of different devices: /device:TPU:1 before, /device:TPU:2 now
where the time goes in v3:
time: 100 us
  Pallas kernels  95.7 us (96%)
  local copies, waits for them, and re-layouts  3.78 us (4%)
    pallas_call x1, Pallas kernels, gather(): pl.pallas_call(gather_kernel, out_shape=(jax.ShapeDtypeStruct((2, NZ, NY...  44 us
    pallas_call x1, Pallas kernels, give_back(): pl.pallas_call(return_kernel, out_shape=(rows, rows), in_specs=[vm, vm],...  35.3 us
    pallas_call x1, Pallas kernels, attention(): pl.pallas_call(attention_kernel, out_shape=(jax.ShapeDtypeStruct((2, LOCA...  16.4 us
    unnamed x6, local copies, waits for them, and re-layouts  2.48 us

profile of v3, /device:TPU:2, one launch (start us, length us, event | category | flops | bytes accessed | tf_op | source)
XLA Modules:
  0.0 100.2 jit_solution(15782730278712864425)
XLA Ops:
  0.6 0.0 copy-start
  0.7 0.8 copy-done
  1.4 0.1 copy.10
  1.6 0.2 reshape.27.rand_ref
  1.8 44.0 %shard_map.93 = (bf16[2,8,128,128]{3,2,1,0:T(8,128)(2,1)}, bf16[2,8,4,2,128,128]{5,4,3,2,1,0:T(8,128)(2,1)}) custom-call(bf16[32,4096]{1,0:T(8,128)(2,1)} %q_ref.1, bf16[32,4096]{1,0:T(8,128)(2,1)} %g_ref.1, bf16[32,4096]{1,0:T(8,128)(2,1)} %k_ref.1, bf16[32,4096]{1,0:T(8,128)(2,1)} %v_ref.1), custom_call_target="tpu_custom_call" | custom-call | tf_op jit(solution)/shard_map/pallas_call | solution.py:198
  45.8 0.0 copy-start.1
  45.8 1.0 %copy-done.1 = bf16[2,8,128,128]{3,2,1,0:T(8,128)(2,1)S(1)} copy-done((bf16[2,8,128,128]{3,2,1,0:T(8,128)(2,1)S(1)}, bf16[2,8,128,128]{3,2,1,0:T(8,128)(2,1)}, u32[]{:S(2)}) %copy-start.1) | copy-done | bytes 524312
  46.8 0.0 copy-start.2
  46.8 0.7 copy-done.2
  47.5 16.4 %shard_map.94 = (bf16[2,1024,128]{2,1,0:T(8,128)(2,1)S(1)}, bf16[2,8192,128]{2,1,0:T(8,128)(2,1)S(1)}) custom-call(s32[384]{0:T(512)S(1)} %reshape.27.rand_ref, s32[2]{0:T(128)S(1)} %copy-done.2, s32[1]{0:T(128)} %bitcast.place_ref, bf16[2,1024,128]{2,1,0:T(8,128)(2,1)S(1)} %bitcast.15, bf16[2,8192,128]{2,1,0:T(8,128)(2,1)} %bitcast.16), custom_call_target="tpu_custom_call" | custom-call | tf_op jit(solution)/shard_map/pallas_call | solution.py:75
  63.9 35.3 %shard_map.95 = (bf16[2,32,4096]{2,1,0:T(8,128)(2,1)S(1)}, bf16[2,32,4096]{2,1,0:T(8,128)(2,1)S(1)}) custom-call(bf16[2,8,128,128]{3,2,1,0:T(8,128)(2,1)S(1)} %bitcast.14, bf16[2,8,4,2,128,128]{5,4,3,2,1,0:T(8,128)(2,1)S(1)} %bitcast.13), custom_call_target="tpu_custom_call" | custom-call | tf_op jit(solution)/shard_map/pallas_call | solution.py:309
  99.2 1.0 slice_bitcast_fusion
  (1 shorter events, 0.0 us)
Async XLA Ops:
  0.6 0.8 copy-start
  45.8 1.0 %copy-start.1 = (bf16[2,8,128,128]{3,2,1,0:T(8,128)(2,1)S(1)}, bf16[2,8,128,128]{3,2,1,0:T(8,128)(2,1)}, u32[]{:S(2)}) copy-start(bf16[2,8,128,128]{3,2,1,0:T(8,128)(2,1)} %get-tuple-element.10) | copy-start | bytes 1572868
  46.8 0.7 copy-start.2

commit v4 on v3

v4 whole, which is shorter than its diff:
```python
import functools
import jax
import jax.numpy as jnp
from jax import lax
from jax.experimental import pallas as pl
from jax.experimental.pallas import tpu as pltpu
from jax.sharding import PartitionSpec as P

HEAD_DIM = 128
BLOCK = 64
SCALE = HEAD_DIM ** -0.5
BLOCKS = 128
LOCAL = 16
NT = (((1,), (1,)), ((), ()))
TN = (((0,), (0,)), ((), ()))
GROUP = 8
NZ, NX, NC, NY = 8, 4, 2, 4


def places():
    return tuple(lax.axis_index(a) for a in ("z", "x", "core", "head"))


def dot(a, b, dims=(((1,), (0,)), ((), ()))):
    return lax.dot_general(a, b, dims, preferred_element_type=jnp.float32)


def attention_kernel(rand_hbm, glob_hbm, qg_ref, kv_ref, out_ref, dkv_ref, acc, rand_ref, glob_ref, sems):
    tables = [
        pltpu.make_async_copy(rand_hbm, rand_ref, sems.at[0]),
        pltpu.make_async_copy(glob_hbm, glob_ref, sems.at[1]),
    ]
    for table in tables:
        table.start()
    z, x, c, y = places()
    head = z * NY + y
    place = x * NC + c

    def clear(t, carry):
        rows = pl.ds(pl.multiple_of(t * 512, 512), 512)
        for n in range(2):
            acc[n, rows, :] = jnp.zeros((512, HEAD_DIM), jnp.float32)
        return carry

    lax.fori_loop(0, BLOCKS * BLOCK // 512, clear, 0)
    for table in tables:
        table.wait()
    lane = lax.broadcasted_iota(jnp.int32, (1, 8 * BLOCK), 1) // BLOCK

    def starts_of(block):
        names = [
            jnp.maximum(block - 1, 0),
            block,
            jnp.minimum(block + 1, BLOCKS - 1),
            glob_ref[0],
            glob_ref[1],
        ] + [rand_ref[r, head, block] for r in range(3)]
        return [pl.multiple_of(n * BLOCK, BLOCK) for n in names]

    def many(turn, carry):
        locals_ = [turn * GROUP + n for n in range(GROUP)]
        blocks = [(t // 2) * 16 + place * 2 + t % 2 for t in locals_]
        starts = [starts_of(b) for b in blocks]
        rows = [pl.ds(pl.multiple_of(t * BLOCK, BLOCK), BLOCK) for t in locals_]
        R = range(GROUP)
        q = [qg_ref[0, rows[n], :] for n in R]
        g = [qg_ref[1, rows[n], :] for n in R]
        k = [jnp.concatenate([kv_ref[0, pl.ds(s, BLOCK), :] for s in starts[n]], axis=0) for n in R]
        v = [jnp.concatenate([kv_ref[1, pl.ds(s, BLOCK), :] for s in starts[n]], axis=0) for n in R]
        s = [dot(q[n], k[n], NT) for n in R]
        dp = [dot(g[n], v[n], NT) for n in R]
        w, p, o, ds = [], [], [], []
        for n in R:
            gone = ((lane == 0) & (blocks[n] == 0)) | ((lane == 2) & (blocks[n] == BLOCKS - 1))
            t = s[n] * SCALE + jnp.where(gone, -jnp.inf, 0.0)
            e = jnp.exp(t - jnp.max(t, axis=1, keepdims=True))
            p.append(e * (1.0 / jnp.sum(e, axis=1, keepdims=True)))
            w.append(p[n].astype(jnp.bfloat16))
        for n in R:
            o.append(dot(w[n], v[n]).astype(jnp.bfloat16))
        dv = [dot(w[n], g[n], TN) for n in R]
        for n in R:
            delta = jnp.sum(g[n].astype(jnp.float32) * o[n].astype(jnp.float32), axis=1, keepdims=True)
            ds.append((p[n] * (dp[n] - delta)).astype(jnp.bfloat16))
        dq = [dot(ds[n], k[n]) for n in R]
        dk = [dot(ds[n], q[n], TN) for n in R]
        for n in R:
            out_ref[0, rows[n], :] = o[n]
            out_ref[1, rows[n], :] = (SCALE * dq[n]).astype(jnp.bfloat16)
            for i, st in enumerate(starts[n]):
                part = slice(i * BLOCK, (i + 1) * BLOCK)
                acc[0, pl.ds(st, BLOCK), :] += dk[n][part]
                acc[1, pl.ds(st, BLOCK), :] += dv[n][part]
        return carry

    lax.fori_loop(0, LOCAL // GROUP, many, 0)

    def finish(t, carry):
        rows = pl.ds(pl.multiple_of(t * 256, 256), 256)
        dkv_ref[0, rows, :] = (SCALE * acc[0, rows, :]).astype(jnp.bfloat16)
        dkv_ref[1, rows, :] = acc[1, rows, :].astype(jnp.bfloat16)
        return carry

    lax.fori_loop(0, BLOCKS * BLOCK // 256, finish, 0)


def attention(rand, glob, qg, kv):
    vm = pl.BlockSpec(memory_space=pltpu.VMEM)
    hbm = pl.BlockSpec(memory_space=pltpu.HBM)
    return pl.pallas_call(
        attention_kernel,
        out_shape=(
            jax.ShapeDtypeStruct((2, LOCAL * BLOCK, HEAD_DIM), jnp.bfloat16),
            jax.ShapeDtypeStruct((2, BLOCKS * BLOCK, HEAD_DIM), jnp.bfloat16),
        ),
        in_specs=[hbm, hbm, vm, vm],
        out_specs=(vm, vm),
        scratch_shapes=[
            pltpu.VMEM((2, BLOCKS * BLOCK, HEAD_DIM), jnp.float32),
            pltpu.SMEM(rand.shape, jnp.int32),
            pltpu.SMEM(glob.shape, jnp.int32),
            pltpu.SemaphoreType.DMA((2,)),
        ],
        compiler_params=pltpu.CompilerParams(vmem_limit_bytes=20 * 1024 * 1024),
    )(rand, glob, qg, kv)

MESH = pl.DeviceIdType.MESH
ROWS = 32
WIDTH = 4096
LAG1, LAG2 = 4, 8
ORDER = (0, 1, 7, 2, 6, 3, 5, 4)


def greet(z, x, c, y, zs, ys):
    barrier = pltpu.get_barrier_semaphore()

    def hello(zz, xx, cc, yy):
        pl.semaphore_signal(barrier, inc=1, device_id=(zz, xx, cc, yy), device_id_type=MESH)

    hello(z, x, 1 - c, y)
    hello(z, (x + 1) % NX, c, y)
    hello(z, (x + 3) % NX, c, y)

    for n in range(1, NZ * NY):
        hello(zs[n // NY], x, c, ys[n % NY])
    pl.semaphore_wait(barrier, NZ * NY - 1 + 3)


def drain(like, sem):
    pltpu.make_async_copy(like, like, sem).wait()


def gather_kernel(q_ref, g_ref, k_ref, v_ref, qg_ref, kv_ref, stage, stage_sem, out_sem, ring_out_sem,
                  qg_sem, a_sem, l_sem, r_sem, f_sem, s_sem):
    z, x, c, y = places()
    loads = [
        pltpu.make_async_copy(src, stage.at[n], stage_sem.at[n])
        for n, src in ((2, k_ref), (3, v_ref), (0, q_ref), (1, g_ref))
    ]
    for load in loads:
        load.start()
    zs = [(z + d) % NZ for d in range(NZ)]
    ys = [(y + d) % NY for d in range(NY)]
    greet(z, x, c, y, zs, ys)
    right, left, over = (x + 1) % NX, (x + 3) % NX, (x + 2) % NX

    def columns(zz, yy):
        return pl.ds(pl.multiple_of((zz * NY + yy) * HEAD_DIM, HEAD_DIM), HEAD_DIM)

    mine = pl.ds(pl.multiple_of(y * ROWS, ROWS), ROWS)

    def scatter(step, first, dst, sem):
        d = ORDER[step]
        for n in range(NY):
            part = stage.at[pl.ds(first, 2), :, columns(zs[d], ys[n])]
            if d == 0 and n == 0:
                pltpu.make_async_copy(part, dst, sem).start()
            else:
                pltpu.make_async_remote_copy(
                    src_ref=part, dst_ref=dst, send_sem=out_sem, recv_sem=sem,
                    device_id=(zs[d], x, c, ys[n]), device_id_type=MESH,
                ).start()

    loads[0].wait()
    loads[1].wait()
    for step in range(NZ):
        scatter(step, 2, kv_ref.at[:, z, x, c, mine, :], a_sem.at[z])
    loads[2].wait()
    loads[3].wait()

    def send(zz, xx, to, sem):
        part = kv_ref.at[:, zz, xx, c]
        pltpu.make_async_remote_copy(
            src_ref=part, dst_ref=part, send_sem=ring_out_sem, recv_sem=sem, device_id=to, device_id_type=MESH,
        ).start()

    to_right, to_left, to_twin = (z, right, c, y), (z, left, c, y), (z, x, 1 - c, y)
    source = [zs[(NZ - d) % NZ] for d in ORDER]
    for step in range(NZ + LAG2):
        if step < NZ:
            zz = source[step]
            drain(kv_ref.at[:, zz, x, c], a_sem.at[zz])
            send(zz, x, to_right, l_sem.at[zz])
            send(zz, x, to_left, r_sem.at[zz])
            send(zz, x, to_twin, s_sem)
            scatter(step, 0, qg_ref.at[:, z, mine, :], qg_sem)
        if LAG1 <= step < NZ + LAG1:
            k = step - LAG1
            zz = source[k]
            drain(kv_ref.at[:, zz, left, c], l_sem.at[zz])
            if k % 2 == 1:
                send(zz, left, to_right, f_sem.at[zz])
            send(zz, left, to_twin, s_sem)
            drain(kv_ref.at[:, zz, right, c], r_sem.at[zz])
            if k % 2 == 0:
                send(zz, right, to_left, f_sem.at[zz])
            send(zz, right, to_twin, s_sem)
        if step >= LAG2:
            zz = source[step - LAG2]
            drain(kv_ref.at[:, zz, over, c], f_sem.at[zz])
            send(zz, over, to_twin, s_sem)
    drain(kv_ref.at[:, :, :, 1 - c], s_sem)
    drain(qg_ref, qg_sem)
    drain(stage.at[:, :, pl.ds(0, (NZ * NY - 1) * HEAD_DIM)], out_sem)
    drain(kv_ref.at[:, pl.ds(0, NZ - 1)], ring_out_sem)


def gather(q, g, k, v):
    anywhere = pl.BlockSpec(memory_space=pl.ANY)
    dma = pltpu.SemaphoreType.DMA
    return pl.pallas_call(
        gather_kernel,
        out_shape=(
            jax.ShapeDtypeStruct((2, NZ, NY * ROWS, HEAD_DIM), jnp.bfloat16),
            jax.ShapeDtypeStruct((2, NZ, NX, NC, NY * ROWS, HEAD_DIM), jnp.bfloat16),
        ),
        in_specs=[pl.BlockSpec(memory_space=pltpu.HBM)] * 4,
        out_specs=(anywhere, anywhere),
        scratch_shapes=[
            pltpu.VMEM((4, ROWS, WIDTH), jnp.bfloat16),
            dma((4,)), dma, dma, dma, dma((NZ,)), dma((NZ,)), dma((NZ,)), dma((NZ,)), dma,
        ],
        compiler_params=pltpu.CompilerParams(
            collective_id=0, has_side_effects=True, vmem_limit_bytes=4 * 1024 * 1024
        ),
    )(q, g, k, v)


BACK1, BACK2 = 3, 6
BACK = (4, 3, 5, 2, 6, 1, 7, 0)


def return_kernel(od_ref, part_ref, od_out, kv_out, twin, sums, hop, joined, from_left, from_right, final,
                  twin_out, ring_out, od_send, kv_send, twin_sem, hop_sem, l_sem, r_sem, od_sem, kv_sem):
    z, x, c, y = places()
    zs = [(z + d) % NZ for d in range(NZ)]
    ys = [(y + d) % NY for d in range(NY)]
    greet(z, x, c, y, zs, ys)
    right, left, over = (x + 1) % NX, (x + 3) % NX, (x + 2) % NX
    planes = [zs[d] for d in BACK]
    columns = pl.ds(pl.multiple_of((z * NY + y) * HEAD_DIM, HEAD_DIM), HEAD_DIM)
    for step in range(NZ):
        pltpu.make_async_remote_copy(
            src_ref=part_ref.at[:, planes[step], :, 1 - c], dst_ref=twin.at[step], send_sem=twin_out,
            recv_sem=twin_sem.at[step], device_id=(z, x, 1 - c, y), device_id_type=MESH,
        ).start()

    def scatter(step, src, dst, send_sem, sem):
        def rows(yy):
            return src.at[:, pl.ds(pl.multiple_of(yy * ROWS, ROWS), ROWS), :]

        for n in range(NY):
            if BACK[step] == 0 and n == 0:
                pltpu.make_async_copy(rows(y), dst.at[:, :, columns], sem).start()
            else:
                pltpu.make_async_remote_copy(
                    src_ref=rows(ys[n]), dst_ref=dst.at[:, :, columns], send_sem=send_sem, recv_sem=sem,
                    device_id=(planes[step], x, c, ys[n]), device_id_type=MESH,
                ).start()

    for step in range(NZ):
        scatter(step, od_ref.at[:, planes[step]], od_out, od_send, od_sem)

    def pass_on(src, dst, sem, xx):
        pltpu.make_async_remote_copy(
            src_ref=src, dst_ref=dst, send_sem=ring_out, recv_sem=sem, device_id=(z, xx, c, y), device_id_type=MESH,
        ).start()

    def wide(a):
        return a.astype(jnp.float32)

    for step in range(NZ + BACK2):
        if step < NZ:
            drain(twin.at[step], twin_sem.at[step])

            def add(xx, carry, step=step):
                for n in range(2):
                    both = wide(part_ref[n, planes[step], xx, c]) + wide(twin[step, n, xx])
                    sums[step, n, xx] = both.astype(jnp.bfloat16)
                return carry

            lax.fori_loop(0, NX, add, 0)
            if step % 2 == 0:
                pass_on(sums.at[step, :, over], hop.at[step], hop_sem.at[step], right)
                pass_on(sums.at[step, :, left], from_right.at[step], r_sem.at[step], left)
            else:
                pass_on(sums.at[step, :, over], hop.at[step], hop_sem.at[step], left)
                pass_on(sums.at[step, :, right], from_left.at[step], l_sem.at[step], right)
        if BACK1 <= step < NZ + BACK1:
            k = step - BACK1
            drain(hop.at[k], hop_sem.at[k])
            to = right if k % 2 == 0 else left
            for n in range(2):
                joined[k, n] = (wide(sums[k, n, to]) + wide(hop[k, n])).astype(jnp.bfloat16)
            if k % 2 == 0:
                pass_on(joined.at[k], from_left.at[k], l_sem.at[k], right)
            else:
                pass_on(joined.at[k], from_right.at[k], r_sem.at[k], left)
        if step >= BACK2:
            k = step - BACK2
            drain(from_left.at[k], l_sem.at[k])
            drain(from_right.at[k], r_sem.at[k])
            for n in range(2):
                total = wide(sums[k, n, x]) + wide(from_left[k, n]) + wide(from_right[k, n])
                final[k, n] = total.astype(jnp.bfloat16)
            scatter(k, final.at[k], kv_out, kv_send, kv_sem)
    drain(part_ref.at[:, :, :, 0], twin_out)
    drain(sums.at[:, :, pl.ds(0, NX - 1)], ring_out)
    others = pl.ds(0, (NZ * NY - 1) * HEAD_DIM)
    drain(od_out.at[:, :, others], od_send)
    drain(kv_out.at[:, :, others], kv_send)
    drain(od_out, od_sem)
    drain(kv_out, kv_sem)


def give_back(od, part):
    hbm = pl.BlockSpec(memory_space=pl.ANY)
    vm = pl.BlockSpec(memory_space=pltpu.VMEM)
    dma = pltpu.SemaphoreType.DMA
    rows = jax.ShapeDtypeStruct((2, ROWS, WIDTH), jnp.bfloat16)
    chunk = pltpu.VMEM((NZ, 2, NY * ROWS, HEAD_DIM), jnp.bfloat16)
    wide_chunk = pltpu.VMEM((NZ, 2, NX, NY * ROWS, HEAD_DIM), jnp.bfloat16)
    each = dma((NZ,))
    return pl.pallas_call(
        return_kernel,
        out_shape=(rows, rows),
        in_specs=[vm, vm],
        out_specs=(hbm, hbm),
        scratch_shapes=[wide_chunk, wide_chunk] + [chunk] * 5 + [dma] * 4 + [each] * 4 + [dma, dma],
        compiler_params=pltpu.CompilerParams(
            collective_id=1, has_side_effects=True, vmem_limit_bytes=20 * 1024 * 1024
        ),
    )(od, part)


def body(queries, keys, values, grad_out, random_blocks, global_blocks):
    rand = jnp.transpose(random_blocks, (2, 0, 1))
    qg, kv = gather(queries, grad_out, keys, values)
    qg = qg.reshape(2, LOCAL * BLOCK, HEAD_DIM)
    kv = kv.reshape(2, BLOCKS * BLOCK, HEAD_DIM)
    od, part = attention(rand, global_blocks, qg, kv)
    od, dkv = give_back(
        od.reshape(2, NZ, NY * ROWS, HEAD_DIM), part.reshape(2, NZ, NX, NC, NY * ROWS, HEAD_DIM)
    )
    return od[0], od[1], dkv[0], dkv[1]


def solution(mesh):
    fine = jax.sharding.Mesh(mesh.devices.reshape(NZ, NX, NC, NY), ("z", "x", "core", "head"))
    rows = P(("z", "x", "core", "head"), None)
    return jax.shard_map(
        body,
        mesh=fine,
        in_specs=(rows, rows, rows, rows, P(), P()),
        out_specs=(rows, rows, rows, rows),
        check_vma=False,
    )
```

time: 100 us -> 83.3 us (0.83)
  the two profiles are of different devices: /device:TPU:2 before, /device:TPU:1 now
where the time goes in v4:
time: 83.3 us; the launch traced here: 83 us
  Pallas kernels  76.1 us (91%)
  local copies, waits for them, and re-layouts  6.22 us (7%)
    pallas_call x1, Pallas kernels, gather(): pl.pallas_call(gather_kernel, out_shape=(jax.ShapeDtypeStruct((2, NZ, NY...  37.4 us
    pallas_call x1, Pallas kernels, give_back(): pl.pallas_call(return_kernel, out_shape=(rows, rows), in_specs=[vm, vm],...  32.7 us
    pallas_call x1, Pallas kernels, attention(): pl.pallas_call(attention_kernel, out_shape=(jax.ShapeDtypeStruct((2, LOCA...  6.03 us
    unnamed x12, local copies, waits for them, and re-layouts  5.24 us

profile of v4, /device:TPU:1, one launch (start us, length us, event | category | flops | bytes accessed | tf_op | source)
XLA Modules:
  0.0 83.0 jit_solution(3974214722685479753)
XLA Ops:
  0.6 0.0 copy-start
  0.6 0.9 %copy-done = bf16[32,4096]{1,0:T(8,128)(2,1)S(1)} copy-done((bf16[32,4096]{1,0:T(8,128)(2,1)S(1)}, bf16[32,4096]{1,0:T(8,128)(2,1)}, u32[]{:S(2)}) %copy-start) | copy-done | bytes 262168
  1.6 0.0 copy-start.1
  1.6 0.9 %copy-done.1 = bf16[32,4096]{1,0:T(8,128)(2,1)S(1)} copy-done((bf16[32,4096]{1,0:T(8,128)(2,1)S(1)}, bf16[32,4096]{1,0:T(8,128)(2,1)}, u32[]{:S(2)}) %copy-start.1) | copy-done | bytes 262168
  2.5 0.0 copy-start.2
  2.5 0.9 %copy-done.2 = bf16[32,4096]{1,0:T(8,128)(2,1)S(1)} copy-done((bf16[32,4096]{1,0:T(8,128)(2,1)S(1)}, bf16[32,4096]{1,0:T(8,128)(2,1)}, u32[]{:S(2)}) %copy-start.2) | copy-done | bytes 262168
  3.5 0.0 copy-start.3
  3.5 0.9 %copy-done.3 = bf16[32,4096]{1,0:T(8,128)(2,1)S(1)} copy-done((bf16[32,4096]{1,0:T(8,128)(2,1)S(1)}, bf16[32,4096]{1,0:T(8,128)(2,1)}, u32[]{:S(2)}) %copy-start.3) | copy-done | bytes 262168
  4.4 37.4 %shard_map.93 = (bf16[2,8,128,128]{3,2,1,0:T(8,128)(2,1)S(1)}, bf16[2,8,4,2,128,128]{5,4,3,2,1,0:T(8,128)(2,1)S(1)}) custom-call(bf16[32,4096]{1,0:T(8,128)(2,1)S(1)} %copy-done, bf16[32,4096]{1,0:T(8,128)(2,1)S(1)} %copy-done.1, bf16[32,4096]{1,0:T(8,128)(2,1)S(1)} %copy-done.2, bf16[32,4096]{1,0:T(8,128)(2,1)S(1)} %copy-done.3), custom_call_target="tpu_custom_call" | custom-call | tf_op jit(solution)/shard_map/pallas_call | solution.py:231
  41.8 0.0 copy-start.4
  41.8 0.8 copy-done.4
  42.6 0.0 copy-start.5
  42.6 0.7 copy-done.5
  43.3 6.0 %shard_map.94 = (bf16[2,1024,128]{2,1,0:T(8,128)(2,1)S(1)}, bf16[2,8192,128]{2,1,0:T(8,128)(2,1)S(1)}) custom-call(s32[3,32,128]{2,1,0:T(8,128)S(1)} %bitcast.17, s32[2]{0:T(128)S(1)} %copy-done.5, bf16[2,1024,128]{2,1,0:T(8,128)(2,1)S(1)} %bitcast.16, bf16[2,8192,128]{2,1,0:T(8,128)(2,1)S(1)} %bitcast.14), custom_call_target="tpu_custom_call" | custom-call | tf_op jit(solution)/shard_map/pallas_call | solution.py:110
  49.3 32.7 %shard_map.95 = (bf16[2,32,4096]{2,1,0:T(8,128)(2,1)S(1)}, bf16[2,32,4096]{2,1,0:T(8,128)(2,1)S(1)}) custom-call(bf16[2,8,128,128]{3,2,1,0:T(8,128)(2,1)S(1)} %bitcast.15, bf16[2,8,4,2,128,128]{5,4,3,2,1,0:T(8,128)(2,1)S(1)} %bitcast.13), custom_call_target="tpu_custom_call" | custom-call | tf_op jit(solution)/shard_map/pallas_call | solution.py:344
  82.0 1.0 %slice_bitcast_fusion = (bf16[32,4096]{1,0:T(8,128)(2,1)}, bf16[32,4096]{1,0:T(8,128)(2,1)}, bf16[32,4096]{1,0:T(8,128)(2,1)}, bf16[32,4096]{1,0:T(8,128)(2,1)}) fusion(bf16[2,32,4096]{2,1,0:T(8,128)(2,1)S(1)} %get-tuple-element.15, bf16[2,32,4096]{2,1,0:T(8,128)(2,1)S(1)} %get-tuple-element.14), kind=kLoop, calls=%fused_computation | loop fusion | bytes 2097152 | tf_op jit(solution)/shard_map/squeeze | solution.py:365
Async XLA Ops:
  0.6 1.0 %copy-start = (bf16[32,4096]{1,0:T(8,128)(2,1)S(1)}, bf16[32,4096]{1,0:T(8,128)(2,1)}, u32[]{:S(2)}) copy-start(bf16[32,4096]{1,0:T(8,128)(2,1)} %q_ref.1) | copy-start | bytes 786436
  1.6 0.9 %copy-start.1 = (bf16[32,4096]{1,0:T(8,128)(2,1)S(1)}, bf16[32,4096]{1,0:T(8,128)(2,1)}, u32[]{:S(2)}) copy-start(bf16[32,4096]{1,0:T(8,128)(2,1)} %g_ref.1) | copy-start | bytes 786436
  2.5 0.9 %copy-start.2 = (bf16[32,4096]{1,0:T(8,128)(2,1)S(1)}, bf16[32,4096]{1,0:T(8,128)(2,1)}, u32[]{:S(2)}) copy-start(bf16[32,4096]{1,0:T(8,128)(2,1)} %k_ref.1) | copy-start | bytes 786436
  3.5 0.9 %copy-start.3 = (bf16[32,4096]{1,0:T(8,128)(2,1)S(1)}, bf16[32,4096]{1,0:T(8,128)(2,1)}, u32[]{:S(2)}) copy-start(bf16[32,4096]{1,0:T(8,128)(2,1)} %v_ref.1) | copy-start | bytes 786436
  41.8 0.8 copy-start.4
  42.6 0.7 copy-start.5

commit v5 on v4

--- a/solution.py
+++ b/solution.py
@@ -122,7 +122,7 @@
             pltpu.SemaphoreType.DMA((2,)),
         ],
         compiler_params=pltpu.CompilerParams(vmem_limit_bytes=20 * 1024 * 1024),
-    )(rand, glob, qg, kv)
+    )(*(pltpu.with_memory_space_constraint(a, pltpu.HBM) for a in (rand, glob)), qg, kv)
 
 MESH = pl.DeviceIdType.MESH
 ROWS = 32
@@ -243,10 +243,10 @@
         compiler_params=pltpu.CompilerParams(
             collective_id=0, has_side_effects=True, vmem_limit_bytes=4 * 1024 * 1024
         ),
-    )(q, g, k, v)
-
-
-BACK1, BACK2 = 3, 6
+    )(*(pltpu.with_memory_space_constraint(a, pltpu.HBM) for a in (q, g, k, v)))
+
+
+BACK1, BACK2 = 2, 4
 BACK = (4, 3, 5, 2, 6, 1, 7, 0)
 
 

time: 83.3 us -> 77.6 us (0.932)
  local copies, waits for them, and re-layouts: 6.22 us -> 0.98 us
    unnamed x12 -> x0, local copies, waits for them, and re-layouts: 5.24 us -> none
where the time goes in v5:
time: 77.6 us; the launch traced here: 77.4 us
  Pallas kernels  75.8 us (98%)
  local copies, waits for them, and re-layouts  0.98 us (1%)
    pallas_call x1, Pallas kernels, gather(): pl.pallas_call(gather_kernel, out_shape=(jax.ShapeDtypeStruct((2, NZ, NY...  37.5 us
    pallas_call x1, Pallas kernels, give_back(): pl.pallas_call(return_kernel, out_shape=(rows, rows), in_specs=[vm, vm],...  32.2 us
    pallas_call x1, Pallas kernels, attention(): pl.pallas_call(attention_kernel, out_shape=(jax.ShapeDtypeStruct((2, LOCA...  6.15 us

profile of v5, /device:TPU:1, one launch (start us, length us, event | category | flops | bytes accessed | tf_op | source)
XLA Modules:
  0.0 77.4 jit_solution(10878603140426672563)
XLA Ops:
  0.6 37.5 %shard_map.93 = (bf16[2,8,128,128]{3,2,1,0:T(8,128)(2,1)S(1)}, bf16[2,8,4,2,128,128]{5,4,3,2,1,0:T(8,128)(2,1)S(1)}) custom-call(bf16[32,4096]{1,0:T(8,128)(2,1)} %q_ref.1, bf16[32,4096]{1,0:T(8,128)(2,1)} %g_ref.1, bf16[32,4096]{1,0:T(8,128)(2,1)} %k_ref.1, bf16[32,4096]{1,0:T(8,128)(2,1)} %v_ref.1), custom_call_target="tpu_custom_call" | custom-call | tf_op jit(solution)/shard_map/pallas_call | solution.py:231
  38.1 6.2 %shard_map.94 = (bf16[2,1024,128]{2,1,0:T(8,128)(2,1)S(1)}, bf16[2,8192,128]{2,1,0:T(8,128)(2,1)S(1)}) custom-call(s32[3,32,128]{2,1,0:T(8,128)} %bitcast.17, s32[2]{0:T(128)} %glob_hbm.1, bf16[2,1024,128]{2,1,0:T(8,128)(2,1)S(1)} %bitcast.16, bf16[2,8192,128]{2,1,0:T(8,128)(2,1)S(1)} %bitcast.14), custom_call_target="tpu_custom_call" | custom-call | tf_op jit(solution)/shard_map/pallas_call | solution.py:110
  44.3 32.2 %shard_map.95 = (bf16[2,32,4096]{2,1,0:T(8,128)(2,1)S(1)}, bf16[2,32,4096]{2,1,0:T(8,128)(2,1)S(1)}) custom-call(bf16[2,8,128,128]{3,2,1,0:T(8,128)(2,1)S(1)} %bitcast.15, bf16[2,8,4,2,128,128]{5,4,3,2,1,0:T(8,128)(2,1)S(1)} %bitcast.13), custom_call_target="tpu_custom_call" | custom-call | tf_op jit(solution)/shard_map/pallas_call | solution.py:344
  76.5 1.0 %slice_bitcast_fusion = (bf16[32,4096]{1,0:T(8,128)(2,1)}, bf16[32,4096]{1,0:T(8,128)(2,1)}, bf16[32,4096]{1,0:T(8,128)(2,1)}, bf16[32,4096]{1,0:T(8,128)(2,1)}) fusion(bf16[2,32,4096]{2,1,0:T(8,128)(2,1)S(1)} %get-tuple-element.15, bf16[2,32,4096]{2,1,0:T(8,128)(2,1)S(1)} %get-tuple-element.14), kind=kLoop, calls=%fused_computation | loop fusion | bytes 2097152 | tf_op jit(solution)/shard_map/squeeze | solution.py:365

commit v6 on v1

v6 whole, which is shorter than its diff:
```python
import functools
import jax
import jax.numpy as jnp
from jax import lax
from jax.experimental import pallas as pl
from jax.experimental.pallas import tpu as pltpu
from jax.sharding import PartitionSpec as P

HEAD_DIM = 128
BLOCK = 64
SCALE = HEAD_DIM ** -0.5
BLOCKS = 128
MESH = pl.DeviceIdType.MESH
NZ, NX, NC, NY = 8, 4, 2, 4
ROWS = 32
WIDTH = 4096
ORDER = (0, 1, 7, 2, 6, 3, 5, 4)
BACK = (4, 3, 5, 2, 6, 1, 7, 0)
QORDER = (4, 3, 5, 2, 6, 1, 7, 0)
LAG1, LAG2 = 4, 8
BACK1, BACK2 = 2, 4
TURN = 4
NEAR = 4
RANDS = 3
WINDOW_TERMS = NZ * NEAR
TERMS = WINDOW_TERMS + NZ * 2 * RANDS + 2
FAR = 1000
NT = (((1,), (1,)), ((), ()))
TN = (((0,), (0,)), ((), ()))


def dot(a, b, dims=(((1,), (0,)), ((), ()))):
    return lax.dot_general(a, b, dims, preferred_element_type=jnp.float32)


def wide(a):
    return a.astype(jnp.float32)


def narrow(a):
    return a.astype(jnp.bfloat16)


def places():
    return tuple(lax.axis_index(a) for a in ("z", "x", "core", "head"))


def greet(z, x, c, y, zs, ys):
    barrier = pltpu.get_barrier_semaphore()

    def hello(zz, xx, cc, yy):
        pl.semaphore_signal(barrier, inc=1, device_id=(zz, xx, cc, yy), device_id_type=MESH)

    hello(z, x, 1 - c, y)
    hello(z, (x + 1) % NX, c, y)
    hello(z, (x + 3) % NX, c, y)
    for n in range(1, NZ * NY):
        hello(zs[n // NY], x, c, ys[n % NY])
    pl.semaphore_wait(barrier, NZ * NY - 1 + 3)


def drain(like, sem):
    pltpu.make_async_copy(like, like, sem).wait()


def columns(zz, yy):
    return pl.ds(pl.multiple_of((zz * NY + yy) * HEAD_DIM, HEAD_DIM), HEAD_DIM)


def quarter(yy):
    return pl.ds(pl.multiple_of(yy * ROWS, ROWS), ROWS)


def layer_kernel(rand_hbm, glob_hbm, q_ref, g_ref, k_ref, v_ref, od_out, dkv_out,
                 stage, kv, qg, od, terms, total, table, twin_send, twin, sums, hop, joined, from_left, from_right, final,
                 rand, glob, picks, small_sem, stage_sem, out_sem, ring_out_sem, qg_sem, a_sem, l_sem, r_sem, f_sem, s_sem,
                 twin_out, back_out, od_send, kv_send, twin_sem, hop_sem, bl_sem, br_sem, od_sem, kv_sem):
    z, x, c, y = places()
    zs = [(z + d) % NZ for d in range(NZ)]
    ys = [(y + d) % NY for d in range(NY)]
    right, left, over = (x + 1) % NX, (x + 3) % NX, (x + 2) % NX
    place = x * NC + c
    head = z * NY + y
    loads = [
        pltpu.make_async_copy(src, stage.at[n], stage_sem.at[n])
        for n, src in ((2, k_ref), (3, v_ref), (0, q_ref), (1, g_ref))
    ]
    small = [
        pltpu.make_async_copy(rand_hbm, rand, small_sem.at[0]),
        pltpu.make_async_copy(glob_hbm, glob, small_sem.at[1]),
    ]
    for load in loads + small:
        load.start()
    greet(z, x, c, y, zs, ys)

    def scatter(d, first, dst, sem):
        for n in range(NY):
            part = stage.at[pl.ds(first, 2), :, columns(zs[d], ys[n])]
            if d == 0 and n == 0:
                pltpu.make_async_copy(part, dst, sem).start()
            else:
                pltpu.make_async_remote_copy(
                    src_ref=part, dst_ref=dst, send_sem=out_sem, recv_sem=sem,
                    device_id=(zs[d], x, c, ys[n]), device_id_type=MESH,
                ).start()

    def chunk(zz, xx, cc):
        return kv.at[:, pl.ds(zz * 16 + xx * 4 + cc * 2, 2)]

    loads[0].wait()
    loads[1].wait()
    for d in ORDER:
        scatter(d, 2, kv.at[:, z * 16 + place * 2 + y // 2, quarter(y % 2), :], a_sem.at[z])

    small[0].wait()
    small[1].wait()
    lane = lax.broadcasted_iota(jnp.int32, (HEAD_DIM, HEAD_DIM), 1)
    row = lax.broadcasted_iota(jnp.int32, (HEAD_DIM, HEAD_DIM), 0)

    def names(slot):
        out = jnp.where(slot < WINDOW_TERMS, slot // NEAR * 16 + place * 2 - 1 + slot % NEAR, FAR)
        for plane in range(NZ):
            for n in range(2):
                for r in range(RANDS):
                    at = WINDOW_TERMS + (plane * 2 + n) * RANDS + r
                    out = jnp.where(slot == at, rand[r, head, plane * 16 + place * 2 + n], out)
        for n in range(2):
            out = jnp.where(slot == TERMS - 2 + n, glob[n], out)
        return out

    down = names(row)
    across = jnp.broadcast_to(names(lax.broadcasted_iota(jnp.int32, (1, HEAD_DIM), 1)), (HEAD_DIM, HEAD_DIM))
    ahead = (across < down) | ((across == down) & (lane < row))
    rank = jnp.sum(jnp.where(ahead, 1, 0), axis=1, keepdims=True)
    table[...] = jnp.zeros((8, HEAD_DIM), jnp.int32)
    table[0:1, :] = jnp.sum(jnp.where(rank == lane, row, 0), axis=0, keepdims=True)
    table[1:2, :] = jnp.sum(jnp.where(down < lane, 1, 0), axis=0, keepdims=True)
    table[2:3, :] = jnp.sum(jnp.where(down < lane + 1, 1, 0), axis=0, keepdims=True)
    picked = pltpu.make_async_copy(table, picks, small_sem.at[0])
    picked.start()
    terms[TERMS - 2] = jnp.zeros((2, BLOCK, HEAD_DIM), jnp.float32)
    terms[TERMS - 1] = jnp.zeros((2, BLOCK, HEAD_DIM), jnp.float32)
    picked.wait()
    loads[2].wait()
    loads[3].wait()

    def send(zz, xx, to, sem):
        pltpu.make_async_remote_copy(
            src_ref=chunk(zz, xx, c), dst_ref=chunk(zz, xx, c), send_sem=ring_out_sem, recv_sem=sem,
            device_id=to, device_id_type=MESH,
        ).start()

    to_right, to_left, to_twin = (z, right, c, y), (z, left, c, y), (z, x, 1 - c, y)
    source = [zs[(NZ - d) % NZ] for d in ORDER]
    for step in range(NZ + LAG2):
        if step < NZ:
            zz = source[step]
            drain(chunk(zz, x, c), a_sem.at[zz])
            send(zz, x, to_right, l_sem.at[zz])
            send(zz, x, to_left, r_sem.at[zz])
            send(zz, x, to_twin, s_sem)
            scatter(QORDER[step], 0, qg.at[:, z, quarter(y), :], qg_sem.at[z])
        if LAG1 <= step < NZ + LAG1:
            k = step - LAG1
            zz = source[k]
            drain(chunk(zz, left, c), l_sem.at[zz])
            if k % 2 == 1:
                send(zz, left, to_right, f_sem.at[zz])
            send(zz, left, to_twin, s_sem)
            drain(chunk(zz, right, c), r_sem.at[zz])
            if k % 2 == 0:
                send(zz, right, to_left, f_sem.at[zz])
            send(zz, right, to_twin, s_sem)
        if step >= LAG2:
            zz = source[step - LAG2]
            drain(chunk(zz, over, c), f_sem.at[zz])
            send(zz, over, to_twin, s_sem)
    drain(kv.at[:, pl.ds(0, BLOCKS // 2)], s_sem)

    def give(d, src, dst, send_sem, sem):
        for n in range(NY):
            part = src.at[:, quarter(ys[n]), :]
            if d == 0 and n == 0:
                pltpu.make_async_copy(part, dst.at[:, :, columns(z, y)], sem).start()
            else:
                pltpu.make_async_remote_copy(
                    src_ref=part, dst_ref=dst.at[:, :, columns(z, y)], send_sem=send_sem, recv_sem=sem,
                    device_id=(zs[d], x, c, ys[n]), device_id_type=MESH,
                ).start()

    shared = (NEAR + 2) * BLOCK
    every = shared + RANDS * BLOCK
    pair = 2 * BLOCK
    which = lax.broadcasted_iota(jnp.int32, (pair, every), 1) // BLOCK
    second = lax.broadcasted_iota(jnp.int32, (pair, every), 0) // BLOCK
    planes = [zs[d] for d in BACK]
    for turn in range(NZ // TURN):
        R = range(TURN)
        group = [planes[turn * TURN + n] for n in R]
        q, g, k, v, kr, vr = [], [], [], [], [], []
        for p in group:
            drain(qg.at[:, p], qg_sem.at[p])
            q.append(qg[0, p])
            g.append(qg[1, p])
            first = p * 16 + place * 2
            near = [(first + BLOCKS - 1) % BLOCKS, first, first + 1, (first + 2) % BLOCKS, glob[0], glob[1]]
            far = [[rand[r, head, first + n] for r in range(RANDS)] for n in range(2)]
            k.append(jnp.concatenate([kv[0, b] for b in near], axis=0))
            v.append(jnp.concatenate([kv[1, b] for b in near], axis=0))
            kr.append([jnp.concatenate([kv[0, b] for b in f], axis=0) for f in far])
            vr.append([jnp.concatenate([kv[1, b] for b in f], axis=0) for f in far])

        def halves(a):
            return a[:BLOCK], a[BLOCK:]

        def against(a, b, br):
            alone = jnp.concatenate([dot(h, m, NT) for h, m in zip(halves(a), br)], axis=0)
            return jnp.concatenate([dot(a, b, NT), alone], axis=1)

        def gathered(a, b, br):
            alone = jnp.concatenate([dot(h, m) for h, m in zip(halves(a[:, shared:]), br)], axis=0)
            return dot(a[:, :shared], b) + alone

        s = [against(q[n], k[n], kr[n]) for n in R]
        dp = [against(g[n], v[n], vr[n]) for n in R]
        p_, w, o, ds = [], [], [], []
        for n in R:
            first = group[n] * 16 + place * 2
            gone = (which == 0) & ((second == 1) | (first == 0))
            gone = gone | ((which == 3) & ((second == 0) | (first == BLOCKS - 2)))
            t = jnp.where(gone, -jnp.inf, s[n] * SCALE)
            e = jnp.exp(t - jnp.max(t, axis=1, keepdims=True))
            p_.append(e * (1.0 / jnp.sum(e, axis=1, keepdims=True)))
            w.append(narrow(p_[n]))
        for n in R:
            o.append(narrow(gathered(w[n], v[n], vr[n])))
        for n in R:
            delta = jnp.sum(wide(g[n]) * wide(o[n]), axis=1, keepdims=True)
            ds.append(narrow(p_[n] * (dp[n] - delta)))
        for n in R:
            p = group[n]
            for kind, left_, right_, scale in ((0, ds[n], q[n], SCALE), (1, w[n], g[n], 1.0)):
                both = dot(left_[:, :shared], right_, TN)
                for i in range(NEAR):
                    terms[p * NEAR + i, kind] = scale * both[i * BLOCK:(i + 1) * BLOCK]
                for i in range(2):
                    terms[TERMS - 2 + i, kind] += scale * both[(NEAR + i) * BLOCK:(NEAR + i + 1) * BLOCK]
                for h, (a, b) in enumerate(zip(halves(left_[:, shared:]), halves(right_))):
                    alone = scale * dot(a, b, TN)
                    for r in range(RANDS):
                        at = WINDOW_TERMS + (p * 2 + h) * RANDS + r
                        terms[at, kind] = alone[r * BLOCK:(r + 1) * BLOCK]
        for n in R:
            od[group[n], 0] = o[n]
            od[group[n], 1] = narrow(SCALE * gathered(ds[n], k[n], kr[n]))
            give(BACK[turn * TURN + n], od.at[group[n]], od_out, od_send, od_sem)

    total[0] = jnp.zeros((2, BLOCK, HEAD_DIM), jnp.float32)

    def run(n, carry):
        at = picks[0, n]
        carry = (carry[0] + terms[at, 0], carry[1] + terms[at, 1])
        total[n + 1, 0] = carry[0]
        total[n + 1, 1] = carry[1]
        return carry

    nothing = jnp.zeros((BLOCK, HEAD_DIM), jnp.float32)
    lax.fori_loop(0, TERMS, run, (nothing, nothing))

    def partial(kind, zz, xx, cc, half):
        block = zz * 16 + xx * 4 + cc * 2 + half
        return total[picks[2, block], kind] - total[picks[1, block], kind]

    for step in range(NZ):
        def fill(xx, carry, step=step):
            for kind in range(2):
                for half in range(2):
                    twin_send[step, kind, xx, half * BLOCK:(half + 1) * BLOCK, :] = narrow(
                        partial(kind, planes[step], xx, 1 - c, half)
                    )
            return carry

        lax.fori_loop(0, NX, fill, 0)
        pltpu.make_async_remote_copy(
            src_ref=twin_send.at[step], dst_ref=twin.at[step], send_sem=twin_out, recv_sem=twin_sem.at[step],
            device_id=to_twin, device_id_type=MESH,
        ).start()

    def pass_on(src, dst, sem, to):
        pltpu.make_async_remote_copy(
            src_ref=src, dst_ref=dst, send_sem=back_out, recv_sem=sem, device_id=to, device_id_type=MESH,
        ).start()

    for step in range(NZ + BACK2):
        if step < NZ:
            drain(twin.at[step], twin_sem.at[step])

            def add(xx, carry, step=step):
                for kind in range(2):
                    for half in range(2):
                        rows = slice(half * BLOCK, (half + 1) * BLOCK)
                        sums[step, kind, xx, rows, :] = narrow(
                            partial(kind, planes[step], xx, c, half) + wide(twin[step, kind, xx, rows, :])
                        )
                return carry

            lax.fori_loop(0, NX, add, 0)
            if step % 2 == 0:
                pass_on(sums.at[step, :, over], hop.at[step], hop_sem.at[step], to_right)
                pass_on(sums.at[step, :, left], from_right.at[step], br_sem.at[step], to_left)
            else:
                pass_on(sums.at[step, :, over], hop.at[step], hop_sem.at[step], to_left)
                pass_on(sums.at[step, :, right], from_left.at[step], bl_sem.at[step], to_right)
        if BACK1 <= step < NZ + BACK1:
            k = step - BACK1
            drain(hop.at[k], hop_sem.at[k])
            to = right if k % 2 == 0 else left
            for n in range(2):
                joined[k, n] = narrow(wide(sums[k, n, to]) + wide(hop[k, n]))
            if k % 2 == 0:
                pass_on(joined.at[k], from_left.at[k], bl_sem.at[k], to_right)
            else:
                pass_on(joined.at[k], from_right.at[k], br_sem.at[k], to_left)
        if step >= BACK2:
            k = step - BACK2
            drain(from_left.at[k], bl_sem.at[k])
            drain(from_right.at[k], br_sem.at[k])
            for n in range(2):
                final[k, n] = narrow(wide(sums[k, n, x]) + wide(from_left[k, n]) + wide(from_right[k, n]))
            give(BACK[k], final.at[k], dkv_out, kv_send, kv_sem)
    others = pl.ds(0, (NZ * NY - 1) * HEAD_DIM)
    drain(stage.at[:, :, others], out_sem)
    drain(kv.at[:, pl.ds(0, BLOCKS - 16)], ring_out_sem)
    drain(twin_send, twin_out)
    drain(sums.at[:, :, pl.ds(0, NX - 1)], back_out)
    drain(od_out.at[:, :, others], od_send)
    drain(dkv_out.at[:, :, others], kv_send)
    drain(od_out, od_sem)
    drain(dkv_out, kv_sem)


def layer(rand, glob, q, g, k, v):
    dma = pltpu.SemaphoreType.DMA
    hbm = pl.BlockSpec(memory_space=pltpu.HBM)
    anywhere = pl.BlockSpec(memory_space=pl.ANY)
    rows = jax.ShapeDtypeStruct((2, ROWS, WIDTH), jnp.bfloat16)
    half = jnp.bfloat16
    plane = pltpu.VMEM((NZ, 2, NY * ROWS, HEAD_DIM), half)
    planes = pltpu.VMEM((NZ, 2, NX, NY * ROWS, HEAD_DIM), half)
    each = dma((NZ,))
    return pl.pallas_call(
        layer_kernel,
        out_shape=(rows, rows),
        in_specs=[hbm] * 6,
        out_specs=(anywhere, anywhere),
        scratch_shapes=[
            pltpu.VMEM((4, ROWS, WIDTH), half),
            pltpu.VMEM((2, BLOCKS, BLOCK, HEAD_DIM), half),
            pltpu.VMEM((2, NZ, NY * ROWS, HEAD_DIM), half),
            plane,
            pltpu.VMEM((TERMS, 2, BLOCK, HEAD_DIM), jnp.float32),
            pltpu.VMEM((TERMS + 1, 2, BLOCK, HEAD_DIM), jnp.float32),
            pltpu.VMEM((8, HEAD_DIM), jnp.int32),
            planes, planes, planes, plane, plane, plane, plane, plane,
            pltpu.SMEM(rand.shape, jnp.int32),
            pltpu.SMEM(glob.shape, jnp.int32),
            pltpu.SMEM((8, HEAD_DIM), jnp.int32),
            dma((2,)), dma((4,)), dma, dma, each, each, each, each, each, dma,
            dma, dma, dma, dma, each, each, each, each, dma, dma,
        ],
        compiler_params=pltpu.CompilerParams(
            collective_id=0, has_side_effects=True, vmem_limit_bytes=48 * 1024 * 1024
        ),
    )(*(pltpu.with_memory_space_constraint(a, pltpu.HBM) for a in (rand, glob, q, g, k, v)))


def body(queries, keys, values, grad_out, random_blocks, global_blocks):
    rand = jnp.transpose(random_blocks, (2, 0, 1))
    od, dkv = layer(rand, global_blocks, queries, grad_out, keys, values)
    return od[0], od[1], dkv[0], dkv[1]


def solution(mesh):
    fine = jax.sharding.Mesh(mesh.devices.reshape(NZ, NX, NC, NY), ("z", "x", "core", "head"))
    rows = P(("z", "x", "core", "head"), None)
    return jax.shard_map(
        body,
        mesh=fine,
        in_specs=(rows, rows, rows, rows, P(), P()),
        out_specs=(rows, rows, rows, rows),
        check_vma=False,
    )
```

time: 210 us -> 72.9 us (0.35)
  blocking collectives: 126 us -> 0 us
  Pallas kernels: 16.4 us -> 70.7 us
  waiting for transfers between devices: 34 us -> 0 us
  between operations: 14.2 us -> 0.64 us
  local copies, waits for them, and re-layouts: 13.6 us -> 0.98 us
  other arithmetic: 3.18 us -> 0 us
    all_to_all x3 -> x0, blocking collectives: 126 us -> none  [the longest x1 52.8 us: body(): lax.all_to_all(dkv, ('x', 'core'), split_axis=0, concat_axis=0, tiled=True)]
    pallas_call x1, Pallas kernels: 16.4 us -> 70.7 us  [layer(): pl.pallas_call(layer_kernel, out_shape=(rows, rows), in_specs=[hbm] * 6,...]
    all_gather x1 -> x0, waiting for transfers between devices: 34 us -> none  [body(): kv = lax.all_gather(got[2:], ('x', 'core'), axis=0)]
    transpose x1 -> x0, local copies, waits for them, and re-layouts: 4.77 us -> none  [body(): kv.reshape(8, 2, 8, 128, HEAD_DIM).transpose(1, 2, 0, 3, 4)]
    unnamed x8 -> x0, local copies, waits for them, and re-layouts: 3.98 us -> none
    reduce_sum x1 -> x0, other arithmetic: 2.95 us -> none  [body(): dkv = jnp.sum(dkv.astype(jnp.float32), axis=0).astype(jnp.bfloat16)]
  transfers between devices with their start and end apart: 1 -> 0, of which waited for: 1 -> 0; matrix products, arithmetic and copies ran while one was open for 0% -> 0% of each run, Pallas kernels for 0% -> 0%
where the time goes in v6:
time: 72.9 us; the launch traced here: 72.3 us
  Pallas kernels  70.7 us (97%)
  local copies, waits for them, and re-layouts  0.98 us (1%)
    pallas_call x1, Pallas kernels, layer(): pl.pallas_call(layer_kernel, out_shape=(rows, rows), in_specs=[hbm] * 6,...  70.7 us

profile of v6, /device:TPU:1, one launch (start us, length us, event | category | flops | bytes accessed | tf_op | source)
XLA Modules:
  0.0 72.3 jit_solution(7897547747880413271)
XLA Ops:
  0.6 70.7 %shard_map.93 = (bf16[2,32,4096]{2,1,0:T(8,128)(2,1)S(1)}, bf16[2,32,4096]{2,1,0:T(8,128)(2,1)S(1)}) custom-call(s32[3,32,128]{2,1,0:T(8,128)} %bitcast.9, s32[2]{0:T(128)} %glob_hbm.1, bf16[32,4096]{1,0:T(8,128)(2,1)} %q_ref.1, bf16[32,4096]{1,0:T(8,128)(2,1)} %g_ref.1, bf16[32,4096]{1,0:T(8,128)(2,1)} %k_ref.1, bf16[32,4096]{1,0:T(8,128)(2,1)} %v_ref.1), custom_call_target="tpu_custom_call" | custom-call | tf_op jit(solution)/shard_map/pallas_call | solution.py:351
  71.3 1.0 %slice_bitcast_fusion = (bf16[32,4096]{1,0:T(8,128)(2,1)}, bf16[32,4096]{1,0:T(8,128)(2,1)}, bf16[32,4096]{1,0:T(8,128)(2,1)}, bf16[32,4096]{1,0:T(8,128)(2,1)}) fusion(bf16[2,32,4096]{2,1,0:T(8,128)(2,1)S(1)} %get-tuple-element.7, bf16[2,32,4096]{2,1,0:T(8,128)(2,1)S(1)} %get-tuple-element.6), kind=kLoop, calls=%fused_computation | loop fusion | bytes 2097152 | tf_op jit(solution)/shard_map/squeeze | solution.py:380

commit v7 on v6

--- a/solution.py
+++ b/solution.py
@@ -16,9 +16,11 @@
 WIDTH = 4096
 ORDER = (0, 1, 7, 2, 6, 3, 5, 4)
 BACK = (4, 3, 5, 2, 6, 1, 7, 0)
-QORDER = (4, 3, 5, 2, 6, 1, 7, 0)
+QORDER = (3, 5, 2, 6, 4, 1, 7, 0)
 LAG1, LAG2 = 4, 8
 BACK1, BACK2 = 2, 4
+TABLES_AT = 8
+AHEAD = 2
 TURN = 4
 NEAR = 4
 RANDS = 3
@@ -112,37 +114,39 @@
     for d in ORDER:
         scatter(d, 2, kv.at[:, z * 16 + place * 2 + y // 2, quarter(y % 2), :], a_sem.at[z])
 
-    small[0].wait()
-    small[1].wait()
-    lane = lax.broadcasted_iota(jnp.int32, (HEAD_DIM, HEAD_DIM), 1)
-    row = lax.broadcasted_iota(jnp.int32, (HEAD_DIM, HEAD_DIM), 0)
-
-    def names(slot):
-        out = jnp.where(slot < WINDOW_TERMS, slot // NEAR * 16 + place * 2 - 1 + slot % NEAR, FAR)
-        for plane in range(NZ):
-            for n in range(2):
-                for r in range(RANDS):
-                    at = WINDOW_TERMS + (plane * 2 + n) * RANDS + r
-                    out = jnp.where(slot == at, rand[r, head, plane * 16 + place * 2 + n], out)
-        for n in range(2):
-            out = jnp.where(slot == TERMS - 2 + n, glob[n], out)
-        return out
-
-    down = names(row)
-    across = jnp.broadcast_to(names(lax.broadcasted_iota(jnp.int32, (1, HEAD_DIM), 1)), (HEAD_DIM, HEAD_DIM))
-    ahead = (across < down) | ((across == down) & (lane < row))
-    rank = jnp.sum(jnp.where(ahead, 1, 0), axis=1, keepdims=True)
-    table[...] = jnp.zeros((8, HEAD_DIM), jnp.int32)
-    table[0:1, :] = jnp.sum(jnp.where(rank == lane, row, 0), axis=0, keepdims=True)
-    table[1:2, :] = jnp.sum(jnp.where(down < lane, 1, 0), axis=0, keepdims=True)
-    table[2:3, :] = jnp.sum(jnp.where(down < lane + 1, 1, 0), axis=0, keepdims=True)
-    picked = pltpu.make_async_copy(table, picks, small_sem.at[0])
-    picked.start()
-    terms[TERMS - 2] = jnp.zeros((2, BLOCK, HEAD_DIM), jnp.float32)
-    terms[TERMS - 1] = jnp.zeros((2, BLOCK, HEAD_DIM), jnp.float32)
-    picked.wait()
     loads[2].wait()
     loads[3].wait()
+
+    picked = pltpu.make_async_copy(table, picks, small_sem.at[0])
+
+    def order_terms():
+        small[0].wait()
+        small[1].wait()
+        lane = lax.broadcasted_iota(jnp.int32, (HEAD_DIM, HEAD_DIM), 1)
+        row = lax.broadcasted_iota(jnp.int32, (HEAD_DIM, HEAD_DIM), 0)
+
+        def names(slot):
+            out = jnp.where(slot < WINDOW_TERMS, slot // NEAR * 16 + place * 2 - 1 + slot % NEAR, FAR)
+            for plane in range(NZ):
+                for n in range(2):
+                    for r in range(RANDS):
+                        at = WINDOW_TERMS + (plane * 2 + n) * RANDS + r
+                        out = jnp.where(slot == at, rand[r, head, plane * 16 + place * 2 + n], out)
+            for n in range(2):
+                out = jnp.where(slot == TERMS - 2 + n, glob[n], out)
+            return out
+
+        down = names(row)
+        across = jnp.broadcast_to(names(lax.broadcasted_iota(jnp.int32, (1, HEAD_DIM), 1)), (HEAD_DIM, HEAD_DIM))
+        ahead = (across < down) | ((across == down) & (lane < row))
+        rank = jnp.sum(jnp.where(ahead, 1, 0), axis=1, keepdims=True)
+        table[...] = jnp.zeros((8, HEAD_DIM), jnp.int32)
+        table[0:1, :] = jnp.sum(jnp.where(rank == lane, row, 0), axis=0, keepdims=True)
+        table[1:2, :] = jnp.sum(jnp.where(down < lane, 1, 0), axis=0, keepdims=True)
+        table[2:3, :] = jnp.sum(jnp.where(down < lane + 1, 1, 0), axis=0, keepdims=True)
+        picked.start()
+        terms[TERMS - 2] = jnp.zeros((2, BLOCK, HEAD_DIM), jnp.float32)
+        terms[TERMS - 1] = jnp.zeros((2, BLOCK, HEAD_DIM), jnp.float32)
 
     def send(zz, xx, to, sem):
         pltpu.make_async_remote_copy(
@@ -153,6 +157,8 @@
     to_right, to_left, to_twin = (z, right, c, y), (z, left, c, y), (z, x, 1 - c, y)
     source = [zs[(NZ - d) % NZ] for d in ORDER]
     for step in range(NZ + LAG2):
+        if step == TABLES_AT:
+            order_terms()
         if step < NZ:
             zz = source[step]
             drain(chunk(zz, x, c), a_sem.at[zz])
@@ -255,6 +261,8 @@
             od[group[n], 1] = narrow(SCALE * gathered(ds[n], k[n], kr[n]))
             give(BACK[turn * TURN + n], od.at[group[n]], od_out, od_send, od_sem)
 
+    picked.wait()
+
     total[0] = jnp.zeros((2, BLOCK, HEAD_DIM), jnp.float32)
 
     def run(n, carry):
@@ -271,8 +279,8 @@
         block = zz * 16 + xx * 4 + cc * 2 + half
         return total[picks[2, block], kind] - total[picks[1, block], kind]
 
-    for step in range(NZ):
-        def fill(xx, carry, step=step):
+    def fill_twin(step):
+        def fill(xx, carry):
             for kind in range(2):
                 for half in range(2):
                     twin_send[step, kind, xx, half * BLOCK:(half + 1) * BLOCK, :] = narrow(
@@ -286,12 +294,17 @@
             device_id=to_twin, device_id_type=MESH,
         ).start()
 
+    for step in range(AHEAD):
+        fill_twin(step)
+
     def pass_on(src, dst, sem, to):
         pltpu.make_async_remote_copy(
             src_ref=src, dst_ref=dst, send_sem=back_out, recv_sem=sem, device_id=to, device_id_type=MESH,
         ).start()
 
     for step in range(NZ + BACK2):
+        if step < NZ - AHEAD:
+            fill_twin(step + AHEAD)
         if step < NZ:
             drain(twin.at[step], twin_sem.at[step])
 

time: 72.9 us -> 69.8 us (0.957)
  Pallas kernels: 70.7 us -> 68 us
    pallas_call x1, Pallas kernels: 70.7 us -> 68 us  [layer(): pl.pallas_call(layer_kernel, out_shape=(rows, rows), in_specs=[hbm] * 6,...]
where the time goes in v7:
time: 69.8 us; the launch traced here: 69.6 us
  Pallas kernels  68 us (97%)
  local copies, waits for them, and re-layouts  0.98 us (1%)
    pallas_call x1, Pallas kernels, layer(): pl.pallas_call(layer_kernel, out_shape=(rows, rows), in_specs=[hbm] * 6,...  68 us

profile of v7, /device:TPU:1, one launch (start us, length us, event | category | flops | bytes accessed | tf_op | source)
XLA Modules:
  0.0 69.6 jit_solution(8841276848116285550)
XLA Ops:
  0.6 68.0 %shard_map.93 = (bf16[2,32,4096]{2,1,0:T(8,128)(2,1)S(1)}, bf16[2,32,4096]{2,1,0:T(8,128)(2,1)S(1)}) custom-call(s32[3,32,128]{2,1,0:T(8,128)} %bitcast.9, s32[2]{0:T(128)} %glob_hbm.1, bf16[32,4096]{1,0:T(8,128)(2,1)} %q_ref.1, bf16[32,4096]{1,0:T(8,128)(2,1)} %g_ref.1, bf16[32,4096]{1,0:T(8,128)(2,1)} %k_ref.1, bf16[32,4096]{1,0:T(8,128)(2,1)} %v_ref.1), custom_call_target="tpu_custom_call" | custom-call | tf_op jit(solution)/shard_map/pallas_call | solution.py:364
  68.6 1.0 %slice_bitcast_fusion = (bf16[32,4096]{1,0:T(8,128)(2,1)}, bf16[32,4096]{1,0:T(8,128)(2,1)}, bf16[32,4096]{1,0:T(8,128)(2,1)}, bf16[32,4096]{1,0:T(8,128)(2,1)}) fusion(bf16[2,32,4096]{2,1,0:T(8,128)(2,1)S(1)} %get-tuple-element.7, bf16[2,32,4096]{2,1,0:T(8,128)(2,1)S(1)} %get-tuple-element.6), kind=kLoop, calls=%fused_computation | loop fusion | bytes 2097152 | tf_op jit(solution)/shard_map/squeeze | solution.py:393

commit v8 on v7

--- a/solution.py
+++ b/solution.py
@@ -165,7 +165,8 @@
             send(zz, x, to_right, l_sem.at[zz])
             send(zz, x, to_left, r_sem.at[zz])
             send(zz, x, to_twin, s_sem)
-            scatter(QORDER[step], 0, qg.at[:, z, quarter(y), :], qg_sem.at[z])
+            for d in QORDER[2 * step:2 * step + 2]:
+                scatter(d, 0, qg.at[:, z, quarter(y), :], qg_sem.at[z])
         if LAG1 <= step < NZ + LAG1:
             k = step - LAG1
             zz = source[k]

time: 69.8 us -> 69.8 us (level)
  no operation moved by 1% of the time
where the time goes in v8:
time: 69.8 us; the launch traced here: 69.6 us
  Pallas kernels  68 us (97%)
  local copies, waits for them, and re-layouts  0.98 us (1%)
    pallas_call x1, Pallas kernels, layer(): pl.pallas_call(layer_kernel, out_shape=(rows, rows), in_specs=[hbm] * 6,...  68 us

profile of v8, /device:TPU:1, one launch (start us, length us, event | category | flops | bytes accessed | tf_op | source)
XLA Modules:
  0.0 69.6 jit_solution(14292729904879879929)
XLA Ops:
  0.6 68.0 %shard_map.93 = (bf16[2,32,4096]{2,1,0:T(8,128)(2,1)S(1)}, bf16[2,32,4096]{2,1,0:T(8,128)(2,1)S(1)}) custom-call(s32[3,32,128]{2,1,0:T(8,128)} %bitcast.9, s32[2]{0:T(128)} %glob_hbm.1, bf16[32,4096]{1,0:T(8,128)(2,1)} %q_ref.1, bf16[32,4096]{1,0:T(8,128)(2,1)} %g_ref.1, bf16[32,4096]{1,0:T(8,128)(2,1)} %k_ref.1, bf16[32,4096]{1,0:T(8,128)(2,1)} %v_ref.1), custom_call_target="tpu_custom_call" | custom-call | tf_op jit(solution)/shard_map/pallas_call | solution.py:365
  68.6 1.0 %slice_bitcast_fusion = (bf16[32,4096]{1,0:T(8,128)(2,1)}, bf16[32,4096]{1,0:T(8,128)(2,1)}, bf16[32,4096]{1,0:T(8,128)(2,1)}, bf16[32,4096]{1,0:T(8,128)(2,1)}) fusion(bf16[2,32,4096]{2,1,0:T(8,128)(2,1)S(1)} %get-tuple-element.7, bf16[2,32,4096]{2,1,0:T(8,128)(2,1)S(1)} %get-tuple-element.6), kind=kLoop, calls=%fused_computation | loop fusion | bytes 2097152 | tf_op jit(solution)/shard_map/squeeze | solution.py:394

commit v9 on v7

--- a/solution.py
+++ b/solution.py
@@ -258,8 +258,14 @@
                         terms[at, kind] = alone[r * BLOCK:(r + 1) * BLOCK]
         for n in R:
             od[group[n], 0] = o[n]
-            od[group[n], 1] = narrow(SCALE * gathered(ds[n], k[n], kr[n]))
-            give(BACK[turn * TURN + n], od.at[group[n]], od_out, od_send, od_sem)
+
+        def send_rows(turn=turn, group=group, ds=ds, k=k, kr=kr):
+            for n in range(TURN):
+                od[group[n], 1] = narrow(SCALE * gathered(ds[n], k[n], kr[n]))
+                give(BACK[turn * TURN + n], od.at[group[n]], od_out, od_send, od_sem)
+
+        if turn < NZ // TURN - 1:
+            send_rows()
 
     picked.wait()
 
@@ -296,6 +302,7 @@
 
     for step in range(AHEAD):
         fill_twin(step)
+    send_rows()
 
     def pass_on(src, dst, sem, to):
         pltpu.make_async_remote_copy(

time: 69.8 us -> 69.8 us (level)
  no operation moved by 1% of the time
where the time goes in v9:
time: 69.8 us; the launch traced here: 69.7 us
  Pallas kernels  68.1 us (98%)
  local copies, waits for them, and re-layouts  0.98 us (1%)
    pallas_call x1, Pallas kernels, layer(): pl.pallas_call(layer_kernel, out_shape=(rows, rows), in_specs=[hbm] * 6,...  68.1 us

profile of v9, /device:TPU:1, one launch (start us, length us, event | category | flops | bytes accessed | tf_op | source)
XLA Modules:
  0.0 69.7 jit_solution(13769559534455776135)
XLA Ops:
  0.6 68.1 %shard_map.93 = (bf16[2,32,4096]{2,1,0:T(8,128)(2,1)S(1)}, bf16[2,32,4096]{2,1,0:T(8,128)(2,1)S(1)}) custom-call(s32[3,32,128]{2,1,0:T(8,128)} %bitcast.9, s32[2]{0:T(128)} %glob_hbm.1, bf16[32,4096]{1,0:T(8,128)(2,1)} %q_ref.1, bf16[32,4096]{1,0:T(8,128)(2,1)} %g_ref.1, bf16[32,4096]{1,0:T(8,128)(2,1)} %k_ref.1, bf16[32,4096]{1,0:T(8,128)(2,1)} %v_ref.1), custom_call_target="tpu_custom_call" | custom-call | tf_op jit(solution)/shard_map/pallas_call | solution.py:371
  68.8 1.0 %slice_bitcast_fusion = (bf16[32,4096]{1,0:T(8,128)(2,1)}, bf16[32,4096]{1,0:T(8,128)(2,1)}, bf16[32,4096]{1,0:T(8,128)(2,1)}, bf16[32,4096]{1,0:T(8,128)(2,1)}) fusion(bf16[2,32,4096]{2,1,0:T(8,128)(2,1)S(1)} %get-tuple-element.7, bf16[2,32,4096]{2,1,0:T(8,128)(2,1)S(1)} %get-tuple-element.6), kind=kLoop, calls=%fused_computation | loop fusion | bytes 2097152 | tf_op jit(solution)/shard_map/squeeze | solution.py:400
